TPU v7x, 256 devices: a whole 4x4x8 slice. The times are simulated.
256 devices in a mesh: gx: 32 (over y, z_lo, core), gy: 8 (over z_hi, x).
Axes of the slice: x: 4, y: 4, z: 8 (z_hi: 2, z_lo: 4; z = z_hi * 4 + z_lo), core: 2. Of those that a mesh axis runs over, the one named last changes fastest.
Arguments:
- control: bfloat16 [2048, 8, 2048], P('gx', None, 'gy'), may hold values from -6 to 6
- innovation: float32 [2048, 8, 2048], P('gx', None, 'gy'), may hold values from -6 to 6
- obs_weight: float32 [2048, 8, 2048], P('gx', None, 'gy'), may hold values from 0.5 to 4
- courant_x: float32 [2048, 8, 2048], P('gx', None, 'gy'), may hold values from -0.9 to 0.9
- courant_y: float32 [2048, 8, 2048], P('gx', None, 'gy'), may hold values from -0.9 to 0.9
- filter_x: bfloat16 [2048, 2048], P('gx'), may hold values from -3 to 3
- filter_y: bfloat16 [2048, 2048], P('gy'), may hold values from -3 to 3
Outputs:
- end_state: float32 [2048, 8, 2048], P('gx', None, 'gy')
- gradient: float32 [2048, 8, 2048], P('gx', None, 'gy')
All inputs are finite; a program needn't handle non-finite values.
Results may differ from a plain program's by a relative error of at most 0.0029.
Values may be sent and summed in bfloat16 or wider, within the bound.
A program may use at most 128 MiB of HBM per device.

v0:
```python
import jax
import jax.numpy as jnp
from jax import lax
from jax.sharding import PartitionSpec as P


def extended(array, sides, width):
    for axis, dim in sides:
        size, length = (lax.axis_size(axis), array.shape[dim])
        up = [(i, (i + 1) % size) for i in range(size - 1)]
        down = [(j, i) for i, j in up]
        last = lax.slice_in_dim(array, length - width, length, axis=dim)
        initial = lax.slice_in_dim(array, 0, width, axis=dim)
        before = lax.ppermute(last, axis, up)
        after = lax.ppermute(initial, axis, down)
        array = jnp.concatenate([before, array, after], axis=dim)
    return array


def per_device(control, innovation, obs_weight, courant_x, courant_y, filter_x, filter_y):
    columns = filter_x
    smoothed = jnp.einsum(
        "ij,jlc->ilc",
        columns,
        lax.all_gather(control, "gx", axis=0, tiled=True),
        preferred_element_type=jnp.float32,
    ).astype(jnp.bfloat16)
    columns = filter_y
    start_state = jnp.einsum(
        "kc,xlc->xlk",
        columns,
        lax.all_gather(smoothed, "gy", axis=2, tiled=True),
        preferred_element_type=jnp.float32,
    )
    padded = extended(start_state, (("gx", 0), ("gy", 2)), 1)
    end_state = (
        start_state
        - courant_x * (padded[2:, :, 1:-1] - padded[:-2, :, 1:-1]) * 0.5
        - courant_y * (padded[1:-1, :, 2:] - padded[1:-1, :, :-2]) * 0.5
    )
    misfit = obs_weight * (end_state - innovation)
    fluxes = jnp.stack([courant_x * misfit, courant_y * misfit])
    rim_cells = extended(fluxes, (("gx", 1), ("gy", 3)), 1)
    adjoint = (
        misfit
        + 0.5 * (rim_cells[0, 2:, :, 1:-1] - rim_cells[0, :-2, :, 1:-1])
        + 0.5 * (rim_cells[1, 1:-1, :, 2:] - rim_cells[1, 1:-1, :, :-2])
    ).astype(jnp.bfloat16)
    partial_sums = jnp.einsum("kc,xlk->xlc", filter_y, adjoint, preferred_element_type=jnp.float32)
    pulled = lax.psum_scatter(partial_sums, "gy", scatter_dimension=2, tiled=True).astype(
        jnp.bfloat16
    )
    columns = filter_x
    carried = lax.psum_scatter(
        jnp.einsum("ij,ilc->jlc", columns, pulled, preferred_element_type=jnp.float32),
        "gx",
        scatter_dimension=0,
        tiled=True,
    )
    gradient = control.astype(jnp.float32) + carried
    return (end_state, gradient)


def solution(mesh):
    placed = (
        P("gx", None, "gy"),
        P("gx", None, "gy"),
        P("gx", None, "gy"),
        P("gx", None, "gy"),
        P("gx", None, "gy"),
        P("gx", None),
        P("gy", None),
    )
    return jax.shard_map(
        per_device,
        mesh=mesh,
        in_specs=placed,
        out_specs=(P("gx", None, "gy"), P("gx", None, "gy")),
        check_vma=False,
    )
```

profile of v0, /device:TPU:1, one launch (start us, length us, event | category | flops | bytes accessed | tf_op | source)
XLA Modules:
  0.0 575.1 jit_solution(11222078684383102453)
XLA Ops:
  7.2 0.7 all-gather.3.cloned.1.call-update
  8.0 75.3 %all-gather.3.cloned.1.call-done = bf16[2048,8,256]{2,1,0:T(8,128)(2,1)} async-done(((bf16[64,8,256]{2,1,0:T(8,128)(2,1)}), bf16[2048,8,256]{2,1,0:T(8,128)(2,1)}) %all-gather.3.cloned.1.call-update) | async-done | bytes 8388624 | tf_op jit(solution)/shard_map/all_gather | solution.py:25
  83.3 5.1 fusion
  88.4 0.9 copy.24
  89.3 74.3 %all-gather.5.cloned.1.call-done = bf16[64,8,2048]{2,1,0:T(8,128)(2,1)} async-done(((bf16[64,8,256]{2,1,0:T(8,128)(2,1)}), bf16[64,8,2048]{2,1,0:T(8,128)(2,1)}) %all-gather.5.cloned.1.call-update) | async-done | bytes 2097168 | tf_op jit(solution)/shard_map/all_gather | solution.py:32
  163.6 2.3 fusion.4
  166.0 3.7 collective-permute-start.1
  169.8 1.9 collective-permute-start
  171.7 3.0 collective-permute-done
  174.9 1.3 collective-permute-start.2
  176.2 4.0 collective-permute-start.3
  180.2 3.4 collective-permute-done.2
  183.6 1.8 collective-permute-done.3
  185.3 2.4 multiply_bitcast_fusion.1
  187.9 3.4 collective-permute-start.5
  191.3 1.9 collective-permute-start.4
  193.2 3.1 collective-permute-done.4
  196.4 1.0 fusion.28
  197.4 1.3 copy.11
  198.7 1.3 collective-permute-start.6
  200.0 0.3 copy.13
  200.3 4.7 collective-permute-start.7
  205.0 0.3 copy.12
  205.3 0.5 collective-permute-done.7
  205.8 1.1 copy.14
  206.9 1.4 fusion.10
  208.2 2.7 fusion.2
  211.0 143.5 %reduce-scatter.3.cloned.1.call-done = f32[64,8,256]{2,0,1:T(8,128)} async-done(((f32[64,8,2048]{2,0,1:T(8,128)}), f32[64,8,256]{2,0,1:T(8,128)}) %reduce-scatter.3.cloned.1.call-update) | async-done | bytes 524304 | tf_op jit(solution)/shard_map/reduce_scatter | solution.py:50
  354.5 9.1 %convolution_bitcast_fusion = f32[2048,8,256]{0,2,1:T(8,128)} fusion(bf16[64,2048]{1,0:T(8,128)(2,1)S(1)} %copy-done.4, f32[64,8,256]{2,0,1:T(8,128)} %reduce-scatter.3.cloned.1.call-done), kind=kOutput, calls=%fused_computation.2 | convolution fusion | flops 537001984 | bytes 17563648 | tf_op jit(solution)/shard_map/ij,ilc->jlc/dot_general | solution.py:55
  363.6 17.8 %copy.15 = f32[2048,8,256]{2,1,0:T(8,128)} copy(f32[2048,8,256]{0,2,1:T(8,128)} %convolution_bitcast_fusion) | data formatting | bytes 33554432 | tf_op jit(solution)/shard_map/ij,ilc->jlc/dot_general | solution.py:55
  381.4 185.3 %reduce-scatter.5.cloned.1.call-done = f32[64,8,256]{2,1,0:T(8,128)} async-done(((f32[2048,8,256]{2,1,0:T(8,128)}), f32[64,8,256]{2,1,0:T(8,128)}) %reduce-scatter.5.cloned.1.call-update) | async-done | bytes 524304 | tf_op jit(solution)/shard_map/reduce_scatter | solution.py:54
  566.7 1.9 convert_add_fusion
  (26 shorter events, 0.6 us)
Async XLA Ops:
  7.2 156.5 %copy-start = (bf16[256,2048]{1,0:T(8,128)(2,1)S(1)}, bf16[256,2048]{1,0:T(8,128)(2,1)}, u32[]{:S(2)}) copy-start(bf16[256,2048]{1,0:T(8,128)(2,1)} %param.13) | copy-start | bytes 3145732
  7.2 76.1 %all-gather.3.cloned.1.call-start = ((), (), s32[]{:S(2)}) async-start(), calls=%async_computation.2 | async-start | bytes 8650752 | tf_op jit(solution)/shard_map/all_gather | solution.py:25
  7.9 155.7 %all-gather.5.cloned.1.call-start = ((), (), s32[]{:S(2)}) async-start(), calls=%async_computation.3 | async-start | bytes 2359296 | tf_op jit(solution)/shard_map/all_gather | solution.py:32
  89.3 96.1 %copy-start.1 = (f32[64,8,256]{2,1,0:T(8,128)S(1)}, f32[64,8,256]{2,1,0:T(8,128)}, u32[]{:S(2)}) copy-start(f32[64,8,256]{2,1,0:T(8,128)} %param.11) | copy-start | bytes 1572868
  89.3 96.1 %copy-start.3 = (f32[64,8,256]{2,1,0:T(8,128)S(1)}, f32[64,8,256]{2,1,0:T(8,128)}, u32[]{:S(2)}) copy-start(f32[64,8,256]{2,1,0:T(8,128)} %param.10) | copy-start | bytes 1572868
  89.3 265.2 %reduce-scatter.3.cloned.1.call-start = ((), (), s32[]{:S(2)}) async-start(), calls=%async_computation.4 | async-start | bytes 4718592 | tf_op jit(solution)/shard_map/reduce_scatter | solution.py:50
  166.0 5.7 collective-permute-start.1
  169.8 5.0 collective-permute-start
  174.9 8.7 %collective-permute-start.2 = (f32[66,8,1]{2,1,0:T(8,128)S(1)}, f32[66,8,1]{2,1,0:T(8,128)S(1)}, u32[]{:S(2)}, u32[]{:S(2)}) collective-permute-start(f32[66,8,1]{2,1,0:T(8,128)S(1)} %get-tuple-element.11), channel_id=1, source_target_pairs={{1,0},{2,1},{3,2},{4,3},{5,4},{6,5},{7,6},{9,8},{10,9},{11,10},{12... | collective-permute-start | bytes 6344 | tf_op jit(solution)/shard_map/ppermute | solution.py:15
  176.2 9.1 %collective-permute-start.3 = (f32[66,8,1]{2,1,0:T(8,128)S(1)}, f32[66,8,1]{2,1,0:T(8,128)S(1)}, u32[]{:S(2)}, u32[]{:S(2)}) collective-permute-start(f32[66,8,1]{2,1,0:T(8,128)S(1)} %get-tuple-element.12), channel_id=1, source_target_pairs={{0,1},{1,2},{2,3},{3,4},{4,5},{5,6},{6,7},{8,9},{9,10},{10,11},{11... | collective-permute-start | bytes 6344 | tf_op jit(solution)/shard_map/ppermute | solution.py:14
  187.9 5.3 collective-permute-start.5
  191.3 5.1 collective-permute-start.4
  198.7 6.3 %collective-permute-start.6 = (f32[2,66,8,1]{1,2,3,0:T(8,128)S(1)}, f32[2,66,8,1]{1,2,3,0:T(8,128)S(1)}, u32[]{:S(2)}, u32[]{:S(2)}) collective-permute-start(f32[2,66,8,1]{1,2,3,0:T(8,128)S(1)} %copy.11), channel_id=1, source_target_pairs={{1,0},{2,1},{3,2},{4,3},{5,4},{6,5},{7,6},{9,8},{10,9},{11,10},{12... | collective-permute-start | bytes 12680 | tf_op jit(solution)/shard_map/ppermute | solution.py:15
  200.3 5.5 collective-permute-start.7
  210.9 143.6 %copy-start.4 = (bf16[64,2048]{1,0:T(8,128)(2,1)S(1)}, bf16[64,2048]{1,0:T(8,128)(2,1)}, u32[]{:S(2)}) copy-start(bf16[64,2048]{1,0:T(8,128)(2,1)} %param.12) | copy-start | bytes 786436
  210.9 355.8 %reduce-scatter.5.cloned.1.call-start = ((), (), s32[]{:S(2)}) async-start(), calls=%async_computation.5 | async-start | bytes 17301504 | tf_op jit(solution)/shard_map/reduce_scatter | solution.py:54
  381.4 185.3 %copy-start.2 = (bf16[64,8,256]{2,1,0:T(8,128)(2,1)S(1)}, bf16[64,8,256]{2,1,0:T(8,128)(2,1)}, u32[]{:S(2)}) copy-start(bf16[64,8,256]{2,1,0:T(8,128)(2,1)} %param.7) | copy-start | bytes 786436
Sparse Core Ops, SparseCore 0:
  9.9 73.3 all-gather.2
  89.4 74.2 all-gather.4
  211.0 143.3 reduce-scatter.2
  381.6 185.0 reduce-scatter.4
where the time goes:
time: 579 us; the launch traced here: 575 us
  waiting for transfers between devices  491 us (85%)
  local copies, waits for them, and re-layouts  22.8 us (4%)
  starting transfers between devices  22.5 us (4%)
  matrix products  19.2 us (3%)
  between operations  13.9 us (2%)
  other arithmetic  5.88 us (1%)
    reduce_scatter x1, waiting for transfers between devices, per_device(): lax.psum_scatter(jnp.einsum('ij,ilc->jlc', columns, pulled, preferred_ele...  185 us
    reduce_scatter x1, waiting for transfers between devices, per_device(): lax.psum_scatter(partial_sums, 'gy', scatter_dimension=2, tiled=True)  143 us
    all_gather x1, waiting for transfers between devices, per_device(): lax.all_gather(control, 'gx', axis=0, tiled=True)  75.3 us
    all_gather x1, waiting for transfers between devices, per_device(): lax.all_gather(smoothed, 'gy', axis=2, tiled=True)  74.3 us
    dot_general x1, local copies, waits for them, and re-layouts, per_device(): jnp.einsum('ij,ilc->jlc', columns, pulled, preferred_element_type=jnp.flo...  17.8 us
    ppermute x4, starting transfers between devices, extended(): before = lax.ppermute(last, axis, up)  15.9 us
  transfers between devices with their start and end apart: 12, of which 9 were waited for; matrix products, arithmetic and copies ran while one was open for 0% of the time, Pallas kernels for 0%

commit v1 on v0

v1 whole, which is shorter than its diff:
```python
import jax
import jax.numpy as jnp
from jax import lax
from jax.experimental import pallas as pl
from jax.experimental.pallas import tpu as pltpu
from jax.sharding import PartitionSpec as P

MESH = pl.DeviceIdType.MESH
F32 = jnp.float32
BF16 = jnp.bfloat16
STEP = {1: 1, 2: 2, 3: 7}


def place(x, y, z, c):
    return (y * 8 + lax.rem(z, 4) * 2 + c, (z // 4) * 4 + x)


def kernel(
    ctl, innov, weight, cou_x, cou_y, fx, fy,
    end_out, grad_out,
    ctl_v, inn_v, wei_v, cx_v, cy_v, end_v, grad_v,
    nat, snd0, cg, fxb, fyb, acc1, s1b, s1g, acc2, s2b, stg,
    st, hys, hyr, hl, hr, qx, py, mis, adj, hps, hpr, ags, ag,
    psend, pown, pg, pb, gsend, gown, gg, gs, go,
    loc_sem, f1_s, f1_r, fo_s, fo_r, f2_s, f2_r, fr_s, fr_r,
    g1_s, g1_r, g2_s, g2_r, gr_s, gr_r,
    s0_s, s0_r, s1_s, s1_r, s2_s, s2_r, s3_s, s3_r,
    h_s, h_r, k_s, k_r, s5_s, s5_r, s6_s, s6_r, s7_s, s7_r, s8_s, s8_r,
):
    gx = lax.axis_index("gx")
    gy = lax.axis_index("gy")
    y = gx // 8
    zl = lax.rem(gx // 2, 4)
    c = lax.rem(gx, 2)
    zh = gy // 4
    x = lax.rem(gy, 4)
    z = zh * 4 + zl
    o = 1 - c
    sib = place(x, y, z, o)
    e = y * 2 + c
    pending = []

    def send(src, dst, ssem, rsem, dev):
        copy = pltpu.make_async_remote_copy(
            src_ref=src, dst_ref=dst, send_sem=ssem, recv_sem=rsem,
            device_id=dev, device_id_type=MESH)
        copy.start()
        pending.append(copy)

    def arrived(dst, rsem):
        pltpu.make_async_copy(dst, dst, rsem).wait()

    xs = [lax.rem(x + t, 4) for t in range(4)]
    ys = [lax.rem(y + t, 4) for t in range(4)]
    zs = [lax.rem(z + t, 8) for t in range(8)]
    up = (lax.rem(gx + 1, 32), gy)
    down = (lax.rem(gx + 31, 32), gy)
    right = (gx, lax.rem(gy + 1, 8))
    left = (gx, lax.rem(gy + 7, 8))

    load_ctl = pltpu.make_async_copy(ctl, ctl_v, loc_sem.at[0])
    load_ctl.start()
    loads = [
        pltpu.make_async_copy(s, d, loc_sem.at[1 + i])
        for i, (s, d) in enumerate([
            (fx, fxb.at[c, 0]), (fy, fyb.at[zh]), (innov, inn_v),
            (weight, wei_v), (cou_x, cx_v), (cou_y, cy_v)])
    ]
    for load in loads:
        load.start()

    barrier = pltpu.get_barrier_semaphore()
    partners = [sib]
    for t in range(1, 8):
        partners += [place(x, y, zs[t], c), place(x, y, zs[t], o)]
    for t in range(1, 4):
        partners += [place(xs[t], y, z, c), place(xs[t], y, z, o)]
        partners += [place(x, ys[t], z, c)]
    partners += [up, down, left, right]
    for dev in partners:
        pl.semaphore_signal(barrier, inc=1, device_id=dev, device_id_type=MESH)

    load_ctl.wait()
    for h in range(2):
        nat[h] = ctl_v[:, :, h * 128:(h + 1) * 128].astype(F32).reshape(512, 128)
    for l in range(8):
        for h in range(2):
            snd0[l, :, h * 128:(h + 1) * 128] = nat[h, pl.ds(l, 64, stride=8), :].astype(BF16)

    pl.semaphore_wait(barrier, len(partners))

    slot0 = zl * 2 + c
    for t in (4, 3, 5, 2, 6, 1, 7):
        send(snd0.at[zs[t]], cg.at[gx], s0_s.at[t], s0_r.at[slot0], place(x, y, zs[t], zh))
    own0 = pltpu.make_async_copy(snd0.at[z], cg.at[gx], s0_r.at[slot0])
    far0 = pltpu.make_async_remote_copy(
        src_ref=snd0.at[z], dst_ref=cg.at[gx], send_sem=s0_s.at[0], recv_sem=s0_r.at[slot0],
        device_id=sib, device_id_type=MESH)

    @pl.when(zh == c)
    def _():
        own0.start()

    @pl.when(zh != c)
    def _():
        far0.start()

    for d in (2, 1, 3):
        dest = place(x, y, lax.rem(z + 8 - STEP[d], 8), c)
        send(fx.at[x], fxb.at[c, d, x], f1_s.at[d - 1], f1_r.at[d - 1], dest)
    send(fx, fxb.at[c, 0], fo_s.at[0], fo_r.at[0], sib)

    for s in range(4):
        for cc in range(2):
            arrived(cg.at[y * 8 + 2 * s + cc], s0_r.at[2 * s + cc])
        block = cg.at[pl.ds(y * 8 + 2 * s, 2)]
        for t in (2, 1, 3):
            send(block, block, s1_s.at[t - 1, s], s1_r.at[t - 1, s], place(x, ys[t], z, c))

    for d in range(1, 4):
        arrived(fxb.at[c, d, x], f1_r.at[d - 1])
    quarter = fxb.at[c, pl.ds(1, 3), x]
    for t in (2, 1, 3):
        send(quarter, quarter, f2_s.at[t - 1], f2_r.at[t - 1], place(xs[t], y, z, c))
    send(quarter, quarter, fr_s.at[0], fr_r.at[0], sib)

    send(fy.at[e], fyb.at[zh, e], g1_s.at[0], g1_r.at[0], place(x, y, zs[4], c))

    for t in (3, 1, 2):
        xq = lax.rem(x + 4 - t, 4)
        part = fxb.at[c, pl.ds(1, 3), xq]
        arrived(part, f2_r.at[t - 1])
        send(part, part, fr_s.at[t], fr_r.at[t], sib)

    loads[0].wait()
    loads[1].wait()
    arrived(fxb.at[o, 0], fo_r.at[0])
    for t in range(4):
        xq = lax.rem(x + 4 - t, 4)
        arrived(fxb.at[o, pl.ds(1, 3), xq], fr_r.at[t])

    def rows_dot(q):
        cols = pl.ds(pl.multiple_of(q * 512, 512), 512)
        a = fxb[:, :, :, :, cols].reshape(512, 512)
        b = cg[pl.ds(q * 8, 8)].reshape(512, 256)
        return jnp.dot(a, b, preferred_element_type=F32)

    acc1[...] = rows_dot(y)
    for t in (3, 1, 2):
        yq = lax.rem(y + 4 - t, 4)
        for s in range(4):
            arrived(cg.at[pl.ds(yq * 8 + 2 * s, 2)], s1_r.at[t - 1, s])
        if t != 2:
            acc1[...] += rows_dot(yq)
        else:
            s1b[...] = (acc1[...] + rows_dot(yq)).astype(BF16).reshape(2, 256, 256)

    mine = c * 4 + x
    for t in (2, 1, 3):
        for r in range(2):
            send(s1b.at[r], s1g.at[mine], s2_s.at[t, r], s2_r.at[t, c], place(xs[t], y, z, r))
    send(s1b.at[o], s1g.at[mine], s2_s.at[0, 0], s2_r.at[0, 0], sib)
    s1g[mine] = s1b[c]

    zo = 1 - zh
    arrived(fyb.at[zo, e], g1_r.at[0])
    for t in (2, 1, 3):
        send(fyb.at[zo, e], fyb.at[zo, e], g2_s.at[t - 1], g2_r.at[t - 1], place(x, ys[t], z, c))
    send(fyb.at[zo, e], fyb.at[zo, e], gr_s.at[0], gr_r.at[0], sib)
    for t in (3, 1, 2):
        eq = lax.rem(y + 4 - t, 4) * 2 + c
        arrived(fyb.at[zo, eq], g2_r.at[t - 1])
        send(fyb.at[zo, eq], fyb.at[zo, eq], gr_s.at[t], gr_r.at[t], sib)
    for t in range(4):
        eq = lax.rem(y + 4 - t, 4) * 2 + o
        arrived(fyb.at[zo, eq], gr_r.at[t])

    def cols_dot(q):
        cols = pl.ds(pl.multiple_of(q * 256, 256), 256)
        b = fyb[:, :, :, cols].reshape(512, 256)
        return lax.dot_general(s1g[q], b, (((1,), (1,)), ((), ())), preferred_element_type=F32)

    acc2[...] = cols_dot(mine)
    arrived(s1g.at[o * 4 + x], s2_r.at[0, 0])
    acc2[...] += cols_dot(o * 4 + x)
    for t in (3, 1, 2):
        xq = lax.rem(x + 4 - t, 4)
        for cc in range(2):
            arrived(s1g.at[cc * 4 + xq], s2_r.at[t, cc])
            acc2[...] += cols_dot(cc * 4 + xq)
    for hh in range(2):
        s2b[hh] = acc2[:, hh * 256:(hh + 1) * 256].astype(BF16).reshape(4, 64, 256)

    for t in (4, 3, 5, 2, 6, 1, 7):
        send(s2b.at[zs[t] // 4, t % 4], stg.at[z], s3_s.at[t - 1], s3_r.at[t - 1], place(x, y, zs[t], c))
    stg[z] = s2b[zh, 0]

    def spread(l):
        value = stg[l].astype(F32)
        for h in range(2):
            st[h, pl.ds(8 + l, 64, stride=8), :] = value[:, h * 128:(h + 1) * 128]

    for t in range(1, 8):
        arrived(stg.at[lax.rem(z + 8 - t, 8)], s3_r.at[t - 1])
    for l in range(8):
        spread(l)

    def edges(field, hsend, hrecv, hleft, hright, ssem, rsem, ref_first, ref_last):
        send(ref_first(0), ref_last(1), ssem.at[0], rsem.at[0], down)
        send(ref_last(0), ref_first(1), ssem.at[1], rsem.at[1], up)
        hsend[0] = field(0).T[0:8]
        send(hsend.at[0], hrecv.at[0], ssem.at[2], rsem.at[2], left)
        hsend[1] = field(1).T[120:128]
        send(hsend.at[1], hrecv.at[1], ssem.at[3], rsem.at[3], right)
        arrived(ref_last(1), rsem.at[0])
        arrived(ref_first(1), rsem.at[1])
        arrived(hrecv.at[0], rsem.at[2])
        arrived(hrecv.at[1], rsem.at[3])
        keep_r = jnp.where(gy == 7, 0.0, 1.0).astype(F32)
        keep_l = jnp.where(gy == 0, 0.0, 1.0).astype(F32)
        hright[...] = jnp.broadcast_to(hrecv[0, 0:1, :] * keep_r, (128, 512)).T
        hleft[...] = jnp.broadcast_to(hrecv[1, 7:8, :] * keep_l, (128, 512)).T

    def fringe(ref):
        first = lambda k: ref.at[:, pl.ds(8, 8)] if k == 0 else ref.at[:, pl.ds(0, 8)]
        last = lambda k: ref.at[:, pl.ds(512, 8)] if k == 0 else ref.at[:, pl.ds(520, 8)]
        return first, last

    def clear(ref):
        @pl.when(gx == 0)
        def _():
            ref[:, 0:8, :] = jnp.zeros((2, 8, 128), F32)

        @pl.when(gx == 31)
        def _():
            ref[:, 520:528, :] = jnp.zeros((2, 8, 128), F32)

    first, last = fringe(st)
    edges(lambda h: st[h, 8:520, :], hys, hyr, hl, hr, h_s, h_r, first, last)
    clear(st)
    for load in loads[2:]:
        load.wait()

    lane = lax.broadcasted_iota(jnp.int32, (64, 128), 1)

    def beside(v0, v1, left_halo, right_halo):
        f0, f1 = pltpu.roll(v0, 127, 1), pltpu.roll(v1, 127, 1)
        b0, b1 = pltpu.roll(v0, 1, 1), pltpu.roll(v1, 1, 1)
        after = (jnp.where(lane == 127, f1, f0), jnp.where(lane == 127, right_halo, f1))
        before = (jnp.where(lane == 0, left_halo, b0), jnp.where(lane == 0, b0, b1))
        return before, after

    @pl.loop(0, 8)
    def _(i):
        at = pl.multiple_of(i * 64, 64)
        xr = pl.ds(i * 8, 8)
        v = [st[h, pl.ds(at + 8, 64), :] for h in range(2)]
        before, after = beside(v[0], v[1], hl[pl.ds(at, 64), :], hr[pl.ds(at, 64), :])
        for h in range(2):
            ln = slice(h * 128, (h + 1) * 128)
            cx = cx_v[xr, :, ln].reshape(64, 128)
            cy = cy_v[xr, :, ln].reshape(64, 128)
            prev = st[h, pl.ds(at, 64), :]
            post = st[h, pl.ds(at + 16, 64), :]
            end = v[h] - cx * (post - prev) * 0.5 - cy * (after[h] - before[h]) * 0.5
            end_v[xr, :, ln] = end.reshape(8, 8, 128)
            m = wei_v[xr, :, ln].reshape(64, 128) * (end - inn_v[xr, :, ln].reshape(64, 128))
            mis[h, pl.ds(at, 64), :] = m
            qx[h, pl.ds(at + 8, 64), :] = cx * m
            py[h, pl.ds(at, 64), :] = cy * m

    store_end = pltpu.make_async_copy(end_v, end_out, loc_sem.at[7])
    store_end.start()

    first, last = fringe(qx)
    edges(lambda h: py[h], hps, hpr, hl, hr, k_s, k_r, first, last)
    clear(qx)

    @pl.loop(0, 8)
    def _(i):
        at = pl.multiple_of(i * 64, 64)
        v = [py[h, pl.ds(at, 64), :] for h in range(2)]
        before, after = beside(v[0], v[1], hl[pl.ds(at, 64), :], hr[pl.ds(at, 64), :])
        for h in range(2):
            prev = qx[h, pl.ds(at, 64), :]
            post = qx[h, pl.ds(at + 16, 64), :]
            adj[h, pl.ds(at, 64), :] = (
                mis[h, pl.ds(at, 64), :] + 0.5 * (post - prev) + 0.5 * (after[h] - before[h]))

    for l in range(8):
        for h in range(2):
            ags[l, :, h * 128:(h + 1) * 128] = adj[h, pl.ds(l, 64, stride=8), :].astype(BF16)

    for t in (4, 3, 5, 2, 6, 1, 7):
        send(ags.at[zs[t]], ag.at[zh, (4 - t % 4) % 4], s5_s.at[t - 1], s5_r.at[t - 1], place(x, y, zs[t], c))
    ag[zh, 0] = ags[z]
    for t in range(1, 8):
        zq = lax.rem(z + 8 - t, 8)
        arrived(ag.at[zq // 4, (4 - t % 4) % 4], s5_r.at[t - 1])

    def share(q):
        cols = pl.ds(pl.multiple_of(q * 256, 256), 256)
        total = None
        for hh in range(2):
            a = ag[hh].reshape(256, 256)
            b = fyb[hh, :, :, cols].reshape(256, 256)
            term = jnp.dot(a, b, preferred_element_type=F32)
            total = term if total is None else total + term
        return total

    for t in (2, 1, 3):
        for r in range(2):
            psend[t, r] = share(r * 4 + xs[t]).astype(BF16)
            send(psend.at[t, r], pg.at[t, c], s6_s.at[t, r], s6_r.at[t, c], place(xs[t], y, z, r))
    psend[0, 0] = share(o * 4 + x).astype(BF16)
    send(psend.at[0, 0], pg.at[0, c], s6_s.at[0, 0], s6_r.at[0, 0], sib)
    pown[...] = share(c * 4 + x)
    arrived(pg.at[0, o], s6_r.at[0, 0])
    for t in range(1, 4):
        for cc in range(2):
            arrived(pg.at[t, cc], s6_r.at[t, cc])
    def three(r):
        return pg[1, r].astype(F32) + pg[2, r].astype(F32) + pg[3, r].astype(F32)

    pb[c] = (three(c) + pown[...]).astype(BF16)
    pb[o] = (three(o) + pg[0, o].astype(F32)).astype(BF16)

    def lines(q):
        cols = pl.ds(pl.multiple_of(q * 512, 512), 512)
        a = fxb[:, :, :, :, cols].reshape(512, 512)
        return lax.dot_general(a, pb[...].reshape(512, 256), (((0,), (0,)), ((), ())), preferred_element_type=F32)

    for t in (2, 1, 3):
        gsend[t - 1] = lines(ys[t]).astype(BF16)
        send(gsend.at[t - 1], gg.at[t - 1], s7_s.at[t - 1], s7_r.at[t - 1], place(x, ys[t], z, c))
    gown[...] = lines(y)
    for t in range(1, 4):
        arrived(gg.at[t - 1], s7_r.at[t - 1])
    gs[...] = (gown[...] + gg[0].astype(F32) + gg[1].astype(F32) + gg[2].astype(F32)).astype(BF16).reshape(8, 64, 256)

    for u in (2, 1, 3, 0):
        zq = lax.rem(zl + u, 4)
        for v in range(2):
            cq = o if v else c
            src = gs.at[zq * 2 + cq]
            if u == 0 and v == 0:
                continue
            send(src, go.at[z], s8_s.at[u, v], s8_r.at[z], place(x, y, c * 4 + zq, cq))
    own8 = pltpu.make_async_copy(gs.at[zl * 2 + c], go.at[z], s8_r.at[z])
    far8 = pltpu.make_async_remote_copy(
        src_ref=gs.at[zl * 2 + c], dst_ref=go.at[z], send_sem=s8_s.at[0, 0], recv_sem=s8_r.at[z],
        device_id=place(x, y, c * 4 + zl, c), device_id_type=MESH)

    @pl.when(zh == c)
    def _():
        own8.start()

    @pl.when(zh != c)
    def _():
        far8.start()

    for l in range(8):
        arrived(go.at[l], s8_r.at[l])
    for l in range(8):
        value = go[l].astype(F32)
        for h in range(2):
            nat[h, pl.ds(l, 64, stride=8), :] = value[:, h * 128:(h + 1) * 128]
    for h in range(2):
        ln = slice(h * 128, (h + 1) * 128)
        grad_v[:, :, ln] = ctl_v[:, :, ln].astype(F32) + nat[h].reshape(64, 8, 128)
    store_grad = pltpu.make_async_copy(grad_v, grad_out, loc_sem.at[8])
    store_grad.start()

    for copy in pending:
        copy.wait_send()

    @pl.when(zh != c)
    def _():
        far0.wait_send()
        far8.wait_send()

    store_end.wait()
    store_grad.wait()


def per_device(control, innovation, obs_weight, courant_x, courant_y, filter_x, filter_y):
    dma = lambda *shape: pltpu.SemaphoreType.DMA(shape)
    big = pltpu.VMEM((64, 8, 256), F32)
    half = pltpu.VMEM((2, 512, 128), F32)
    ext = pltpu.VMEM((2, 528, 128), F32)
    col = pltpu.VMEM((512, 128), F32)
    lev = pltpu.VMEM((8, 64, 256), BF16)
    halo = pltpu.VMEM((2, 8, 512), F32)
    scratch = [
        pltpu.VMEM((64, 8, 256), BF16), big, big, big, big, big, big,
        half, lev,
        pltpu.VMEM((32, 64, 256), BF16),
        pltpu.VMEM((2, 4, 4, 16, 2048), BF16),
        pltpu.VMEM((2, 8, 32, 2048), BF16),
        pltpu.VMEM((512, 256), F32),
        pltpu.VMEM((2, 256, 256), BF16),
        pltpu.VMEM((8, 256, 256), BF16),
        pltpu.VMEM((256, 512), F32),
        pltpu.VMEM((2, 4, 64, 256), BF16),
        lev,
        ext, halo, halo, col, col, ext, half, half, half, halo, halo, lev,
        pltpu.VMEM((2, 4, 64, 256), BF16),
        pltpu.VMEM((4, 2, 256, 256), BF16),
        pltpu.VMEM((256, 256), F32),
        pltpu.VMEM((4, 2, 256, 256), BF16),
        pltpu.VMEM((2, 256, 256), BF16),
        pltpu.VMEM((3, 512, 256), BF16),
        pltpu.VMEM((512, 256), F32),
        pltpu.VMEM((3, 512, 256), BF16),
        lev, lev,
        dma(9), dma(3), dma(3), dma(1), dma(1), dma(3), dma(3), dma(4), dma(4),
        dma(1), dma(1), dma(3), dma(3), dma(4), dma(4),
        dma(8), dma(8), dma(3, 4), dma(3, 4), dma(4, 2), dma(4, 2), dma(7), dma(7),
        dma(4), dma(4), dma(4), dma(4), dma(7), dma(7), dma(4, 2), dma(4, 2), dma(3), dma(3), dma(4, 2), dma(8),
    ]
    out = jax.ShapeDtypeStruct((64, 8, 256), F32)
    anywhere = pl.BlockSpec(memory_space=pl.ANY)
    return pl.pallas_call(
        kernel,
        out_shape=(out, out),
        in_specs=[anywhere] * 7,
        out_specs=(anywhere, anywhere),
        scratch_shapes=scratch,
        compiler_params=pltpu.CompilerParams(
            collective_id=0, has_side_effects=True, vmem_limit_bytes=40 * 1024 * 1024),
        cost_estimate=pl.CostEstimate(flops=2150000000, bytes_accessed=5000000, transcendentals=0),
    )(control, innovation, obs_weight, courant_x, courant_y,
      filter_x.reshape(4, 16, 2048), filter_y.reshape(8, 32, 2048))


def solution(mesh):
    grid = P("gx", None, "gy")
    placed = (grid, grid, grid, grid, grid, P("gx", None), P("gy", None))
    return jax.shard_map(
        per_device, mesh=mesh, in_specs=placed, out_specs=(grid, grid), check_vma=False)
```

time: 579 us -> 123 us (0.21)
  waiting for transfers between devices: 491 us -> 0 us
  Pallas kernels: 0 us -> 111 us
  starting transfers between devices: 22.5 us -> 0 us
  matrix products: 19.2 us -> 0 us
  local copies, waits for them, and re-layouts: 22.8 us -> 8.87 us
  between operations: 13.9 us -> 0.66 us
  other arithmetic: 5.88 us -> 0 us
    reduce_scatter x2 -> x0, waiting for transfers between devices: 329 us -> none  [the longest x1 185 us: per_device(): lax.psum_scatter(jnp.einsum('ij,ilc->jlc', columns, pulled, preferred_ele...]
    all_gather x2 -> x0, waiting for transfers between devices: 150 us -> none  [the longest x1 75.3 us: per_device(): lax.all_gather(control, 'gx', axis=0, tiled=True)]
    pallas_call x0 -> x1, Pallas kernels: none -> 111 us  [per_device(): pl.pallas_call(kernel, out_shape=(out, out), in_specs=[anywhere] * 7, out...]
    ppermute x8 -> x0, starting transfers between devices: 22.3 us -> none  [the longest x4 15.9 us: extended(): before = lax.ppermute(last, axis, up)]
    dot_general x4 -> x0, matrix products: 19.2 us -> none  [the longest x1 9.13 us: per_device(): jnp.einsum('ij,ilc->jlc', columns, pulled, preferred_element_type=jnp.flo...]
    dot_general x2 -> x0, local copies, waits for them, and re-layouts: 18.7 us -> none  [the longest x1 17.8 us: per_device(): jnp.einsum('ij,ilc->jlc', columns, pulled, preferred_element_type=jnp.flo...]
    ppermute x8 -> x0, waiting for transfers between devices: 11.7 us -> none  [the longest x4 9.51 us: extended(): after = lax.ppermute(initial, axis, down)]
    unnamed x10 -> x16, local copies, waits for them, and re-layouts: 0.03 us -> 8.87 us
  transfers between devices with their start and end apart: 12 -> 0, of which waited for: 9 -> 0; matrix products, arithmetic and copies ran while one was open for 0% -> 0% of each run, Pallas kernels for 0% -> 0%
where the time goes in v1:
time: 123 us; the launch traced here: 120 us
  Pallas kernels  111 us (90%)
  local copies, waits for them, and re-layouts  8.87 us (7%)
    pallas_call x1, Pallas kernels, per_device(): pl.pallas_call(kernel, out_shape=(out, out), in_specs=[anywhere] * 7, out...  111 us
    unnamed x16, local copies, waits for them, and re-layouts  8.87 us

profile of v1, /device:TPU:1, one launch (start us, length us, event | category | flops | bytes accessed | tf_op | source)
XLA Modules:
  0.0 120.5 jit_solution(5086602485126248926)
XLA Ops:
  0.6 0.0 copy-start
  0.6 1.2 %copy-done = bf16[256,2048]{1,0:T(8,128)(2,1)S(1)} copy-done((bf16[256,2048]{1,0:T(8,128)(2,1)S(1)}, bf16[256,2048]{1,0:T(8,128)(2,1)}, u32[]{:S(2)}) %copy-start) | copy-done | bytes 1048600
  1.9 0.0 copy-start.1
  1.9 1.0 copy-done.1
  2.9 0.0 copy-start.2
  2.9 1.0 copy-done.2
  3.9 0.0 copy-start.3
  3.9 1.0 copy-done.3
  5.0 0.0 copy-start.4
  5.0 1.0 copy-done.4
  6.0 0.0 copy-start.5
  6.0 0.9 copy-done.5
  7.0 0.0 copy-start.6
  7.0 0.9 copy-done.6
  7.9 111.0 %shard_map.86 = (f32[64,8,256]{2,1,0:T(8,128)S(1)}, f32[64,8,256]{2,1,0:T(8,128)S(1)}) custom-call(bf16[64,8,256]{2,1,0:T(8,128)(2,1)S(1)} %copy-done.5, f32[64,8,256]{2,1,0:T(8,128)S(1)} %copy-done.1, f32[64,8,256]{2,1,0:T(8,128)S(1)} %copy-done.2, f32[64,8,256]{2,1,0:T(8,128)S(1)} %copy-done.3, f32[64,8,256]{2,1,0:T(8,128)S(1)} %copy-done.4, ...), custom_call_target="tpu_custom_call" | custom-call | flops 2150000128 | bytes 5000000 | tf_op jit(solution)/shard_map/pallas_call | solution.py:423
  118.9 0.8 copy.11
  119.7 0.8 copy.12
Async XLA Ops:
  0.6 1.2 %copy-start = (bf16[256,2048]{1,0:T(8,128)(2,1)S(1)}, bf16[256,2048]{1,0:T(8,128)(2,1)}, u32[]{:S(2)}) copy-start(bf16[256,2048]{1,0:T(8,128)(2,1)} %param.13) | copy-start | bytes 3145732
  1.9 1.0 copy-start.1
  2.9 1.0 copy-start.2
  3.9 1.0 copy-start.3
  5.0 1.0 copy-start.4
  6.0 0.9 copy-start.5
  7.0 0.9 copy-start.6

commit v2 on v1

v2 whole, which is shorter than its diff:
```python
import jax
import jax.numpy as jnp
from jax import lax
from jax.experimental import pallas as pl
from jax.experimental.pallas import tpu as pltpu
from jax.sharding import PartitionSpec as P

MESH = pl.DeviceIdType.MESH
F32 = jnp.float32
BF16 = jnp.bfloat16
def place(x, y, z, c):
    return (y * 8 + lax.rem(z, 4) * 2 + c, (z // 4) * 4 + x)


def kernel(
    ctl, innov, weight, cou_x, cou_y, fx, fy,
    end_out, grad_out,
    ctl_v, inn_v, wei_v, cx_v, cy_v, end_v, grad_v,
    nat, snd0, cg, fxb, fyb, acc1, s1b, s1g, acc2, s2b, stg,
    st, hys, hyr, hl, hr, qx, py, mis, adj, hps, hpr, ags, ag,
    psend, pown, pg, pb, gsend, gown, gg, gs, go,
    loc_sem, f1_s, f1_r, fo_s, fo_r, f2_s, f2_r, fr_s, fr_r,
    g1_s, g1_r, g2_s, g2_r, gr_s, gr_r,
    s0_s, s0_r, s1_s, s1_r, s2_s, s2_r, s3_s, s3_r,
    h_s, h_r, k_s, k_r, s5_s, s5_r, s6_s, s6_r, s7_s, s7_r, s8_s, s8_r,
):
    gx = lax.axis_index("gx")
    gy = lax.axis_index("gy")
    y = gx // 8
    zl = lax.rem(gx // 2, 4)
    c = lax.rem(gx, 2)
    zh = gy // 4
    x = lax.rem(gy, 4)
    z = zh * 4 + zl
    o = 1 - c
    sib = place(x, y, z, o)
    e = y * 2 + c
    pending = []

    def send(src, dst, ssem, rsem, dev):
        copy = pltpu.make_async_remote_copy(
            src_ref=src, dst_ref=dst, send_sem=ssem, recv_sem=rsem,
            device_id=dev, device_id_type=MESH)
        copy.start()
        pending.append(copy)

    def arrived(dst, rsem):
        pltpu.make_async_copy(dst, dst, rsem).wait()

    xs = [lax.rem(x + t, 4) for t in range(4)]
    ys = [lax.rem(y + t, 4) for t in range(4)]
    zs = [lax.rem(z + t, 8) for t in range(8)]
    up = (lax.rem(gx + 1, 32), gy)
    down = (lax.rem(gx + 31, 32), gy)
    right = (gx, lax.rem(gy + 1, 8))
    left = (gx, lax.rem(gy + 7, 8))

    load_ctl = pltpu.make_async_copy(ctl, ctl_v, loc_sem.at[0])
    load_ctl.start()
    loads = [
        pltpu.make_async_copy(s, d, loc_sem.at[1 + i])
        for i, (s, d) in enumerate([
            (fx, fxb.at[c, 0]), (fy, fyb.at[zh]), (innov, inn_v),
            (weight, wei_v), (cou_x, cx_v), (cou_y, cy_v)])
    ]
    for load in loads:
        load.start()

    barrier = pltpu.get_barrier_semaphore()
    partners = [sib]
    for t in range(1, 8):
        partners += [place(x, y, zs[t], c), place(x, y, zs[t], o)]
    for t in range(1, 4):
        partners += [place(xs[t], y, z, c), place(xs[t], y, z, o)]
        partners += [place(x, ys[t], z, c)]
    partners += [up, down, left, right]
    for dev in partners:
        pl.semaphore_signal(barrier, inc=1, device_id=dev, device_id_type=MESH)

    load_ctl.wait()
    for h in range(2):
        nat[h] = ctl_v[:, :, h * 128:(h + 1) * 128].astype(F32).reshape(512, 128)
    for l in range(8):
        for h in range(2):
            snd0[h, l] = nat[h, pl.ds(l, 64, stride=8), :].astype(BF16)

    pl.semaphore_wait(barrier, len(partners))

    slot0 = zl * 2 + c
    for h in range(2):
        for t in (4, 3, 5, 2, 6, 1, 7):
            send(snd0.at[h, zs[t]], cg.at[h, gx], s0_s.at[h, t], s0_r.at[h, slot0], place(x, y, zs[t], zh))
    own0 = [pltpu.make_async_copy(snd0.at[h, z], cg.at[h, gx], s0_r.at[h, slot0]) for h in range(2)]
    far0 = [pltpu.make_async_remote_copy(
        src_ref=snd0.at[h, z], dst_ref=cg.at[h, gx], send_sem=s0_s.at[h, 0], recv_sem=s0_r.at[h, slot0],
        device_id=sib, device_id_type=MESH) for h in range(2)]

    @pl.when(zh == c)
    def _():
        own0[0].start()
        own0[1].start()

    @pl.when(zh != c)
    def _():
        far0[0].start()
        far0[1].start()

    x2 = xs[2]
    for d, k, q, dz in ((2, 0, x, 6), (2, 1, x2, 2), (1, 0, x, 7), (3, 0, x, 1), (1, 1, x2, 7), (3, 1, x2, 1)):
        send(fx.at[q], fxb.at[c, d, q], f1_s.at[d - 1, k], f1_r.at[d - 1, k], place(x, y, zs[dz], c))
    send(fx, fxb.at[c, 0], fo_s.at[0], fo_r.at[0], sib)

    for h in range(2):
        for s in range(4):
            for cc in range(2):
                arrived(cg.at[h, y * 8 + 2 * s + cc], s0_r.at[h, 2 * s + cc])
            block = cg.at[h, pl.ds(y * 8 + 2 * s, 2)]
            for t in (2, 1, 3):
                send(block, block, s1_s.at[h, t - 1, s], s1_r.at[h, t - 1, s], place(x, ys[t], z, c))

    for d in range(1, 4):
        arrived(fxb.at[c, d, x], f1_r.at[d - 1, 0])
    quarter = fxb.at[c, pl.ds(1, 3), x]
    for t in (1, 3):
        send(quarter, quarter, f2_s.at[t // 2], f2_r.at[t // 2], place(xs[t], y, z, c))
    send(quarter, quarter, fr_s.at[0], fr_r.at[0], sib)
    for d in range(1, 4):
        arrived(fxb.at[c, d, x2], f1_r.at[d - 1, 1])
    quarter = fxb.at[c, pl.ds(1, 3), x2]
    send(quarter, quarter, fr_s.at[2], fr_r.at[2], sib)

    send(fy.at[e], fyb.at[zh, e], g1_s.at[0], g1_r.at[0], place(x, y, zs[4], c))

    for t in (1, 3):
        part = fxb.at[c, pl.ds(1, 3), xs[4 - t]]
        arrived(part, f2_r.at[t // 2])
        send(part, part, fr_s.at[t], fr_r.at[t], sib)

    loads[0].wait()
    loads[1].wait()
    arrived(fxb.at[o, 0], fo_r.at[0])
    for t in range(4):
        arrived(fxb.at[o, pl.ds(1, 3), xs[(4 - t) % 4]], fr_r.at[t])

    def rows_dot(h, q):
        cols = pl.ds(pl.multiple_of(q * 512, 512), 512)
        a = fxb[:, :, :, :, cols].reshape(512, 512)
        b = cg[h, pl.ds(q * 8, 8)].reshape(512, 128)
        return jnp.dot(a, b, preferred_element_type=F32)

    mine = c * 4 + x
    for h in range(2):
        acc1[...] = rows_dot(h, y)
        for t in (3, 1, 2):
            yq = ys[4 - t]
            for s in range(4):
                arrived(cg.at[h, pl.ds(yq * 8 + 2 * s, 2)], s1_r.at[h, t - 1, s])
            if t != 2:
                acc1[...] += rows_dot(h, yq)
            else:
                s1b[h] = (acc1[...] + rows_dot(h, yq)).astype(BF16).reshape(2, 256, 128)
        for k, rows in ((0, pl.ds(0, 256)),) if h == 0 else ((1, pl.ds(0, 128)), (2, pl.ds(128, 128))):
            for t in (2, 1, 3):
                for r in range(2):
                    send(s1b.at[h, r, rows], s1g.at[h, mine, rows],
                         s2_s.at[k, t, r], s2_r.at[k, t, c], place(xs[t], y, z, r))
            send(s1b.at[h, o, rows], s1g.at[h, mine, rows], s2_s.at[k, 0, 0], s2_r.at[k, 0, 0], sib)
        s1g[h, mine] = s1b[h, c]

    zo = 1 - zh
    arrived(fyb.at[zo, e], g1_r.at[0])
    for t in (2, 1, 3):
        send(fyb.at[zo, e], fyb.at[zo, e], g2_s.at[t - 1], g2_r.at[t - 1], place(x, ys[t], z, c))
    send(fyb.at[zo, e], fyb.at[zo, e], gr_s.at[0], gr_r.at[0], sib)

    def cols_dot(h, q, hh, start, size):
        cols = pl.ds(pl.multiple_of(q * 256 + h * 128, 128), 128)
        b = fyb[hh, :, :, cols].reshape(256, 128)
        a = s1g[h, q, start:start + size, :]
        return lax.dot_general(a, b, (((1,), (1,)), ((), ())), preferred_element_type=F32)

    sources = [(0, 0, mine), (0, 0, o * 4 + x)]
    sources += [(t, cc, cc * 4 + xs[4 - t]) for t in (3, 1, 2) for cc in range(2)]
    for i, (t, cc, q) in enumerate(sources):
        if i:
            arrived(s1g.at[0, q], s2_r.at[0, t, cc])
        term = cols_dot(0, q, zh, 0, 256)
        acc2[zh] = acc2[zh] + term if i else term

    for t in (3, 1, 2):
        eq = ys[4 - t] * 2 + c
        arrived(fyb.at[zo, eq], g2_r.at[t - 1])
        send(fyb.at[zo, eq], fyb.at[zo, eq], gr_s.at[t], gr_r.at[t], sib)
    for t in range(4):
        arrived(fyb.at[zo, ys[(4 - t) % 4] * 2 + o], gr_r.at[t])
    for i, (t, cc, q) in enumerate(sources):
        term = cols_dot(0, q, zo, 0, 256)
        acc2[zo] = acc2[zo] + term if i else term

    for g in range(2):
        rows = pl.ds(g * 128, 128)
        for i, (t, cc, q) in enumerate(sources):
            if i:
                arrived(s1g.at[1, q, rows], s2_r.at[1 + g, t, cc])
            for hh in range(2):
                acc2[hh, rows] += cols_dot(1, q, hh, g * 128, 128)
        for hh in range(2):
            s2b[hh, 2 * g:2 * g + 2] = acc2[hh, rows].astype(BF16).reshape(2, 64, 256)
        for t in ((4, 5, 1) if g == 0 else (3, 2, 6, 7)):
            send(s2b.at[zs[t] // 4, t % 4], stg.at[z], s3_s.at[t - 1], s3_r.at[t - 1], place(x, y, zs[t], c))
    stg[z] = s2b[zh, 0]

    def spread(l):
        value = stg[l].astype(F32)
        for h in range(2):
            st[h, pl.ds(8 + l, 64, stride=8), :] = value[:, h * 128:(h + 1) * 128]

    for t in range(1, 8):
        arrived(stg.at[lax.rem(z + 8 - t, 8)], s3_r.at[t - 1])
    for l in range(8):
        spread(l)

    def edges(field, hsend, hrecv, hleft, hright, ssem, rsem, ref_first, ref_last):
        send(ref_first(0), ref_last(1), ssem.at[0], rsem.at[0], down)
        send(ref_last(0), ref_first(1), ssem.at[1], rsem.at[1], up)
        hsend[0] = field(0).T[0:8]
        send(hsend.at[0], hrecv.at[0], ssem.at[2], rsem.at[2], left)
        hsend[1] = field(1).T[120:128]
        send(hsend.at[1], hrecv.at[1], ssem.at[3], rsem.at[3], right)
        arrived(ref_last(1), rsem.at[0])
        arrived(ref_first(1), rsem.at[1])
        arrived(hrecv.at[0], rsem.at[2])
        arrived(hrecv.at[1], rsem.at[3])
        keep_r = jnp.where(gy == 7, 0.0, 1.0).astype(F32)
        keep_l = jnp.where(gy == 0, 0.0, 1.0).astype(F32)
        hright[...] = jnp.broadcast_to(hrecv[0, 0:1, :] * keep_r, (128, 512)).T
        hleft[...] = jnp.broadcast_to(hrecv[1, 7:8, :] * keep_l, (128, 512)).T

    def fringe(ref):
        first = lambda k: ref.at[:, pl.ds(8, 8)] if k == 0 else ref.at[:, pl.ds(0, 8)]
        last = lambda k: ref.at[:, pl.ds(512, 8)] if k == 0 else ref.at[:, pl.ds(520, 8)]
        return first, last

    def clear(ref):
        @pl.when(gx == 0)
        def _():
            ref[:, 0:8, :] = jnp.zeros((2, 8, 128), F32)

        @pl.when(gx == 31)
        def _():
            ref[:, 520:528, :] = jnp.zeros((2, 8, 128), F32)

    first, last = fringe(st)
    edges(lambda h: st[h, 8:520, :], hys, hyr, hl, hr, h_s, h_r, first, last)
    clear(st)
    for load in loads[2:]:
        load.wait()

    lane = lax.broadcasted_iota(jnp.int32, (64, 128), 1)

    def beside(v0, v1, left_halo, right_halo):
        f0, f1 = pltpu.roll(v0, 127, 1), pltpu.roll(v1, 127, 1)
        b0, b1 = pltpu.roll(v0, 1, 1), pltpu.roll(v1, 1, 1)
        after = (jnp.where(lane == 127, f1, f0), jnp.where(lane == 127, right_halo, f1))
        before = (jnp.where(lane == 0, left_halo, b0), jnp.where(lane == 0, b0, b1))
        return before, after

    @pl.loop(0, 8)
    def _(i):
        at = pl.multiple_of(i * 64, 64)
        xr = pl.ds(i * 8, 8)
        v = [st[h, pl.ds(at + 8, 64), :] for h in range(2)]
        before, after = beside(v[0], v[1], hl[pl.ds(at, 64), :], hr[pl.ds(at, 64), :])
        for h in range(2):
            ln = slice(h * 128, (h + 1) * 128)
            cx = cx_v[xr, :, ln].reshape(64, 128)
            cy = cy_v[xr, :, ln].reshape(64, 128)
            prev = st[h, pl.ds(at, 64), :]
            post = st[h, pl.ds(at + 16, 64), :]
            end = v[h] - cx * (post - prev) * 0.5 - cy * (after[h] - before[h]) * 0.5
            end_v[xr, :, ln] = end.reshape(8, 8, 128)
            m = wei_v[xr, :, ln].reshape(64, 128) * (end - inn_v[xr, :, ln].reshape(64, 128))
            mis[h, pl.ds(at, 64), :] = m
            qx[h, pl.ds(at + 8, 64), :] = cx * m
            py[h, pl.ds(at, 64), :] = cy * m

    store_end = pltpu.make_async_copy(end_v, end_out, loc_sem.at[7])
    store_end.start()

    first, last = fringe(qx)
    edges(lambda h: py[h], hps, hpr, hl, hr, k_s, k_r, first, last)
    clear(qx)

    @pl.loop(0, 8)
    def _(i):
        at = pl.multiple_of(i * 64, 64)
        v = [py[h, pl.ds(at, 64), :] for h in range(2)]
        before, after = beside(v[0], v[1], hl[pl.ds(at, 64), :], hr[pl.ds(at, 64), :])
        for h in range(2):
            prev = qx[h, pl.ds(at, 64), :]
            post = qx[h, pl.ds(at + 16, 64), :]
            adj[h, pl.ds(at, 64), :] = (
                mis[h, pl.ds(at, 64), :] + 0.5 * (post - prev) + 0.5 * (after[h] - before[h]))

    for l in range(8):
        for h in range(2):
            ags[l, :, h * 128:(h + 1) * 128] = adj[h, pl.ds(l, 64, stride=8), :].astype(BF16)

    for t in (4, 3, 7, 2, 6, 5, 1):
        send(ags.at[zs[t]], ag.at[zh, (4 - t % 4) % 4], s5_s.at[t - 1], s5_r.at[t - 1], place(x, y, zs[t], c))
    ag[zh, 0] = ags[z]

    def share(g, q):
        cols = pl.ds(pl.multiple_of(q * 256, 256), 256)
        total = None
        for hh in range(2):
            a = ag[hh, 2 * g:2 * g + 2].reshape(128, 256)
            b = fyb[hh, :, :, cols].reshape(256, 256)
            term = jnp.dot(a, b, preferred_element_type=F32)
            total = term if total is None else total + term
        return total

    targets = [(t, r, r * 4 + xs[t], place(xs[t], y, z, r)) for t in (2, 1, 3) for r in range(2)]
    targets += [(0, 0, o * 4 + x, sib)]

    def hand(h, k, rows):
        for t, r, q, dev in targets:
            send(psend.at[h, t, r, rows], pg.at[h, t, c, rows],
                 s6_s.at[k, t, r], s6_r.at[k, t, c], dev)

    for g in range(2):
        rows = pl.ds(g * 128, 128)
        for t in ((4, 3, 7) if g == 0 else (2, 6, 5, 1)):
            arrived(ag.at[zs[8 - t] // 4, (4 - t % 4) % 4], s5_r.at[t - 1])
        for t, r, q, dev in targets:
            value = share(g, q).astype(BF16)
            for h in range(2):
                psend[h, t, r, rows] = value[:, h * 128:(h + 1) * 128]
            send(psend.at[0, t, r, rows], pg.at[0, t, c, rows],
                 s6_s.at[g, t, r], s6_r.at[g, t, c], dev)
        value = share(g, mine)
        for h in range(2):
            pown[h, rows] = value[:, h * 128:(h + 1) * 128]
    hand(1, 2, pl.ds(0, 256))

    def lines(h, q):
        cols = pl.ds(pl.multiple_of(q * 512, 512), 512)
        a = fxb[:, :, :, :, cols].reshape(512, 512)
        b = pb[h].reshape(512, 128)
        return lax.dot_general(a, b, (((0,), (0,)), ((), ())), preferred_element_type=F32)

    def three(h, r):
        return pg[h, 1, r].astype(F32) + pg[h, 2, r].astype(F32) + pg[h, 3, r].astype(F32)

    for h in range(2):
        for k, rows in ((0, pl.ds(0, 128)), (1, pl.ds(128, 128))) if h == 0 else ((2, pl.ds(0, 256)),):
            arrived(pg.at[h, 0, o, rows], s6_r.at[k, 0, o])
            for t in range(1, 4):
                for cc in range(2):
                    arrived(pg.at[h, t, cc, rows], s6_r.at[k, t, cc])
        pb[h, c] = (three(h, c) + pown[h]).astype(BF16)
        pb[h, o] = (three(h, o) + pg[h, 0, o].astype(F32)).astype(BF16)
        for t in (2, 1, 3):
            gsend[h, t - 1] = lines(h, ys[t]).astype(BF16)
            send(gsend.at[h, t - 1], gg.at[h, t - 1], s7_s.at[h, t - 1], s7_r.at[h, t - 1], place(x, ys[t], z, c))
        gown[h] = lines(h, y)

    own8, far8 = [], []
    for h in range(2):
        for t in range(1, 4):
            arrived(gg.at[h, t - 1], s7_r.at[h, t - 1])
        total = gown[h] + gg[h, 0].astype(F32) + gg[h, 1].astype(F32) + gg[h, 2].astype(F32)
        gs[h] = total.astype(BF16).reshape(8, 64, 128)
        for u in (2, 1, 3, 0):
            zq = lax.rem(zl + u, 4)
            for v in range(2):
                cq = o if v else c
                if u or v:
                    send(gs.at[h, zq * 2 + cq], go.at[h, z], s8_s.at[h, u, v], s8_r.at[h, z],
                         place(x, y, c * 4 + zq, cq))
        src, dst = gs.at[h, zl * 2 + c], go.at[h, z]
        own8.append(pltpu.make_async_copy(src, dst, s8_r.at[h, z]))
        far8.append(pltpu.make_async_remote_copy(
            src_ref=src, dst_ref=dst, send_sem=s8_s.at[h, 0, 0], recv_sem=s8_r.at[h, z],
            device_id=place(x, y, c * 4 + zl, c), device_id_type=MESH))

        @pl.when(zh == c)
        def _():
            own8[h].start()

        @pl.when(zh != c)
        def _():
            far8[h].start()

    for h in range(2):
        ln = slice(h * 128, (h + 1) * 128)
        for l in range(8):
            arrived(go.at[h, l], s8_r.at[h, l])
        for l in range(8):
            nat[h, pl.ds(l, 64, stride=8), :] = go[h, l].astype(F32)
        grad_v[:, :, ln] = ctl_v[:, :, ln].astype(F32) + nat[h].reshape(64, 8, 128)
    store_grad = pltpu.make_async_copy(grad_v, grad_out, loc_sem.at[8])
    store_grad.start()

    for copy in pending:
        copy.wait_send()

    @pl.when(zh != c)
    def _():
        for h in range(2):
            far0[h].wait_send()
            far8[h].wait_send()

    store_end.wait()
    store_grad.wait()


def per_device(control, innovation, obs_weight, courant_x, courant_y, filter_x, filter_y):
    dma = lambda *shape: pltpu.SemaphoreType.DMA(shape)
    big = pltpu.VMEM((64, 8, 256), F32)
    half = pltpu.VMEM((2, 512, 128), F32)
    ext = pltpu.VMEM((2, 528, 128), F32)
    col = pltpu.VMEM((512, 128), F32)
    lev = pltpu.VMEM((8, 64, 256), BF16)
    levh = pltpu.VMEM((2, 8, 64, 128), BF16)
    halo = pltpu.VMEM((2, 8, 512), F32)
    planes = pltpu.VMEM((2, 4, 64, 256), BF16)
    shares = pltpu.VMEM((2, 4, 2, 256, 128), BF16)
    sums = pltpu.VMEM((2, 3, 512, 128), BF16)
    scratch = [
        pltpu.VMEM((64, 8, 256), BF16), big, big, big, big, big, big,
        half, levh,
        pltpu.VMEM((2, 32, 64, 128), BF16),
        pltpu.VMEM((2, 4, 4, 16, 2048), BF16),
        pltpu.VMEM((2, 8, 32, 2048), BF16),
        pltpu.VMEM((512, 128), F32),
        pltpu.VMEM((2, 2, 256, 128), BF16),
        pltpu.VMEM((2, 8, 256, 128), BF16),
        pltpu.VMEM((2, 256, 256), F32),
        planes, lev,
        ext, halo, halo, col, col, ext, half, half, half, halo, halo, lev, planes,
        shares,
        pltpu.VMEM((2, 256, 128), F32),
        shares,
        pltpu.VMEM((2, 2, 256, 128), BF16),
        sums,
        pltpu.VMEM((2, 512, 128), F32),
        sums, levh, levh,
        dma(9), dma(3, 2), dma(3, 2), dma(1), dma(1), dma(2), dma(2), dma(4), dma(4),
        dma(1), dma(1), dma(3), dma(3), dma(4), dma(4),
        dma(2, 8), dma(2, 8), dma(2, 3, 4), dma(2, 3, 4), dma(3, 4, 2), dma(3, 4, 2), dma(7), dma(7),
        dma(4), dma(4), dma(4), dma(4), dma(7), dma(7), dma(3, 4, 2), dma(3, 4, 2),
        dma(2, 3), dma(2, 3), dma(2, 4, 2), dma(2, 8),
    ]
    out = jax.ShapeDtypeStruct((64, 8, 256), F32)
    anywhere = pl.BlockSpec(memory_space=pl.ANY)
    return pl.pallas_call(
        kernel,
        out_shape=(out, out),
        in_specs=[anywhere] * 7,
        out_specs=(anywhere, anywhere),
        scratch_shapes=scratch,
        compiler_params=pltpu.CompilerParams(
            collective_id=0, has_side_effects=True, vmem_limit_bytes=60 * 1024 * 1024),
        cost_estimate=pl.CostEstimate(flops=2150000000, bytes_accessed=5000000, transcendentals=0),
    )(control, innovation, obs_weight, courant_x, courant_y,
      filter_x.reshape(4, 16, 2048), filter_y.reshape(8, 32, 2048))


def solution(mesh):
    grid = P("gx", None, "gy")
    placed = (grid, grid, grid, grid, grid, P("gx", None), P("gy", None))
    return jax.shard_map(
        per_device, mesh=mesh, in_specs=placed, out_specs=(grid, grid), check_vma=False)
```

time: 123 us -> 108 us (0.88); the launches traced: 120 us -> 108 us
  Pallas kernels: 111 us -> 104 us
  local copies, waits for them, and re-layouts: 8.87 us -> 2.72 us
    pallas_call x1, Pallas kernels: 111 us -> 104 us  [per_device(): pl.pallas_call(kernel, out_shape=(out, out), in_specs=[anywhere] * 7, out...]
    unnamed x16 -> x4, local copies, waits for them, and re-layouts: 8.87 us -> 2.72 us
where the time goes in v2:
time: 108 us
  Pallas kernels  104 us (96%)
  local copies, waits for them, and re-layouts  2.72 us (3%)
    pallas_call x1, Pallas kernels, per_device(): pl.pallas_call(kernel, out_shape=(out, out), in_specs=[anywhere] * 7, out...  104 us
    unnamed x4, local copies, waits for them, and re-layouts  2.72 us

profile of v2, /device:TPU:1, one launch (start us, length us, event | category | flops | bytes accessed | tf_op | source)
XLA Modules:
  0.0 107.7 jit_solution(6804223159003387322)
XLA Ops:
  0.6 104.3 %shard_map.86 = (f32[64,8,256]{2,1,0:T(8,128)}, f32[64,8,256]{2,1,0:T(8,128)}) custom-call(bf16[64,8,256]{2,1,0:T(8,128)(2,1)} %ctl.1, f32[64,8,256]{2,1,0:T(8,128)} %innov.1, f32[64,8,256]{2,1,0:T(8,128)} %weight.1, f32[64,8,256]{2,1,0:T(8,128)} %cou_x.1, f32[64,8,256]{2,1,0:T(8,128)} %cou_y.1, bf16[4,16,2048]{2,1,0:T(8,128)(2,1)} %bitcast.3, ...), custom_call_target="tpu_custom_call" | custom-call | flops 2150000128 | bytes 5000000 | tf_op jit(solution)/shard_map/pallas_call | solution.py:457
  105.0 0.0 copy-start
  105.0 1.9 %copy.11 = f32[64,8,256]{2,1,0:T(8,128)} copy(f32[64,8,256]{2,1,0:T(8,128)} %get-tuple-element.4) | data formatting | bytes 1048576
  106.9 0.0 copy-done
  106.9 0.8 copy.12
Async XLA Ops:
  105.0 1.9 %copy-start = (f32[64,8,256]{2,1,0:T(8,128)S(1)}, f32[64,8,256]{2,1,0:T(8,128)}, u32[]{:S(2)}) copy-start(f32[64,8,256]{2,1,0:T(8,128)} %get-tuple-element.5) | copy-start | bytes 1572868

commit v3 on v2

--- a/solution.py
+++ b/solution.py
@@ -15,8 +15,8 @@
 def kernel(
     ctl, innov, weight, cou_x, cou_y, fx, fy,
     end_out, grad_out,
-    ctl_v, inn_v, wei_v, cx_v, cy_v, end_v, grad_v,
-    nat, snd0, cg, fxb, fyb, acc1, s1b, s1g, acc2, s2b, stg,
+    ctl_v, inn_v, wei_v, cx_v, cy_v,
+    nat, snd0, cg, fxb, fyb, s1b, s1g, acc2, s2b, stg,
     st, hys, hyr, hl, hr, qx, py, mis, adj, hps, hpr, ags, ag,
     psend, pown, pg, pb, gsend, gown, gg, gs, go,
     loc_sem, f1_s, f1_r, fo_s, fo_r, f2_s, f2_r, fr_s, fr_r,
@@ -105,18 +105,23 @@
         far0[0].start()
         far0[1].start()
 
-    x2 = xs[2]
-    for d, k, q, dz in ((2, 0, x, 6), (2, 1, x2, 2), (1, 0, x, 7), (3, 0, x, 1), (1, 1, x2, 7), (3, 1, x2, 1)):
-        send(fx.at[q], fxb.at[c, d, q], f1_s.at[d - 1, k], f1_r.at[d - 1, k], place(x, y, zs[dz], c))
     send(fx, fxb.at[c, 0], fo_s.at[0], fo_r.at[0], sib)
 
-    for h in range(2):
+    def ring(h):
         for s in range(4):
             for cc in range(2):
                 arrived(cg.at[h, y * 8 + 2 * s + cc], s0_r.at[h, 2 * s + cc])
             block = cg.at[h, pl.ds(y * 8 + 2 * s, 2)]
             for t in (2, 1, 3):
                 send(block, block, s1_s.at[h, t - 1, s], s1_r.at[h, t - 1, s], place(x, ys[t], z, c))
+
+    ring(0)
+
+    x2 = xs[2]
+    for d, k, q, dz in ((2, 0, x, 6), (1, 0, x, 7), (3, 0, x, 1), (2, 1, x2, 2), (1, 1, x2, 7), (3, 1, x2, 1)):
+        send(fx.at[q], fxb.at[c, d, q], f1_s.at[d - 1, k], f1_r.at[d - 1, k], place(x, y, zs[dz], c))
+
+    ring(1)
 
     for d in range(1, 4):
         arrived(fxb.at[c, d, x], f1_r.at[d - 1, 0])
@@ -131,41 +136,38 @@
 
     send(fy.at[e], fyb.at[zh, e], g1_s.at[0], g1_r.at[0], place(x, y, zs[4], c))
 
+    mine = c * 4 + x
+
+    def smooth(d):
+        a = fxb[:, d].reshape(128, 2048)
+        for h in range(2):
+            v = jnp.dot(a, cg[h].reshape(2048, 128), preferred_element_type=F32)
+            s1b[:, d, :, h * 128:(h + 1) * 128] = v.astype(BF16).reshape(2, 64, 128)
+        rows = pl.ds(d * 64, 64)
+        for t in (2, 1, 3):
+            for r in range(2):
+                send(s1b.at[r, d], s1g.at[mine, rows],
+                     s2_s.at[d, t, r], s2_r.at[d, t, c], place(xs[t], y, z, r))
+        send(s1b.at[o, d], s1g.at[mine, rows], s2_s.at[d, 0, 0], s2_r.at[d, 0, 0], sib)
+        s1g[mine, rows] = s1b[c, d]
+
+    for h in range(2):
+        for t in (3, 1, 2):
+            for s in range(4):
+                arrived(cg.at[h, pl.ds(ys[4 - t] * 8 + 2 * s, 2)], s1_r.at[h, t - 1, s])
+    loads[0].wait()
+    loads[1].wait()
+    arrived(fxb.at[o, 0], fo_r.at[0])
+    smooth(0)
     for t in (1, 3):
         part = fxb.at[c, pl.ds(1, 3), xs[4 - t]]
         arrived(part, f2_r.at[t // 2])
         send(part, part, fr_s.at[t], fr_r.at[t], sib)
-
-    loads[0].wait()
-    loads[1].wait()
-    arrived(fxb.at[o, 0], fo_r.at[0])
     for t in range(4):
         arrived(fxb.at[o, pl.ds(1, 3), xs[(4 - t) % 4]], fr_r.at[t])
-
-    def rows_dot(h, q):
-        cols = pl.ds(pl.multiple_of(q * 512, 512), 512)
-        a = fxb[:, :, :, :, cols].reshape(512, 512)
-        b = cg[h, pl.ds(q * 8, 8)].reshape(512, 128)
-        return jnp.dot(a, b, preferred_element_type=F32)
-
-    mine = c * 4 + x
-    for h in range(2):
-        acc1[...] = rows_dot(h, y)
-        for t in (3, 1, 2):
-            yq = ys[4 - t]
-            for s in range(4):
-                arrived(cg.at[h, pl.ds(yq * 8 + 2 * s, 2)], s1_r.at[h, t - 1, s])
-            if t != 2:
-                acc1[...] += rows_dot(h, yq)
-            else:
-                s1b[h] = (acc1[...] + rows_dot(h, yq)).astype(BF16).reshape(2, 256, 128)
-        for k, rows in ((0, pl.ds(0, 256)),) if h == 0 else ((1, pl.ds(0, 128)), (2, pl.ds(128, 128))):
-            for t in (2, 1, 3):
-                for r in range(2):
-                    send(s1b.at[h, r, rows], s1g.at[h, mine, rows],
-                         s2_s.at[k, t, r], s2_r.at[k, t, c], place(xs[t], y, z, r))
-            send(s1b.at[h, o, rows], s1g.at[h, mine, rows], s2_s.at[k, 0, 0], s2_r.at[k, 0, 0], sib)
-        s1g[h, mine] = s1b[h, c]
+    smooth(1)
+    smooth(2)
+    smooth(3)
 
     zo = 1 - zh
     arrived(fyb.at[zo, e], g1_r.at[0])
@@ -173,19 +175,11 @@
         send(fyb.at[zo, e], fyb.at[zo, e], g2_s.at[t - 1], g2_r.at[t - 1], place(x, ys[t], z, c))
     send(fyb.at[zo, e], fyb.at[zo, e], gr_s.at[0], gr_r.at[0], sib)
 
-    def cols_dot(h, q, hh, start, size):
-        cols = pl.ds(pl.multiple_of(q * 256 + h * 128, 128), 128)
-        b = fyb[hh, :, :, cols].reshape(256, 128)
-        a = s1g[h, q, start:start + size, :]
+    def cols_dot(q, hh, g):
+        cols = pl.ds(pl.multiple_of(q * 256, 256), 256)
+        b = fyb[hh, :, :, cols].reshape(256, 256)
+        a = s1g[q, g * 128:(g + 1) * 128, :]
         return lax.dot_general(a, b, (((1,), (1,)), ((), ())), preferred_element_type=F32)
-
-    sources = [(0, 0, mine), (0, 0, o * 4 + x)]
-    sources += [(t, cc, cc * 4 + xs[4 - t]) for t in (3, 1, 2) for cc in range(2)]
-    for i, (t, cc, q) in enumerate(sources):
-        if i:
-            arrived(s1g.at[0, q], s2_r.at[0, t, cc])
-        term = cols_dot(0, q, zh, 0, 256)
-        acc2[zh] = acc2[zh] + term if i else term
 
     for t in (3, 1, 2):
         eq = ys[4 - t] * 2 + c
@@ -193,19 +187,22 @@
         send(fyb.at[zo, eq], fyb.at[zo, eq], gr_s.at[t], gr_r.at[t], sib)
     for t in range(4):
         arrived(fyb.at[zo, ys[(4 - t) % 4] * 2 + o], gr_r.at[t])
-    for i, (t, cc, q) in enumerate(sources):
-        term = cols_dot(0, q, zo, 0, 256)
-        acc2[zo] = acc2[zo] + term if i else term
+    sources = [(0, 0, mine), (0, 0, o * 4 + x)]
+    sources += [(t, cc, cc * 4 + xs[4 - t]) for t in (3, 1, 2) for cc in range(2)]
 
     for g in range(2):
-        rows = pl.ds(g * 128, 128)
         for i, (t, cc, q) in enumerate(sources):
             if i:
-                arrived(s1g.at[1, q, rows], s2_r.at[1 + g, t, cc])
+                for d in (2 * g, 2 * g + 1):
+                    arrived(s1g.at[q, pl.ds(d * 64, 64)], s2_r.at[d, t, cc])
             for hh in range(2):
-                acc2[hh, rows] += cols_dot(1, q, hh, g * 128, 128)
-        for hh in range(2):
-            s2b[hh, 2 * g:2 * g + 2] = acc2[hh, rows].astype(BF16).reshape(2, 64, 256)
+                term = cols_dot(q, hh, g)
+                if i == 0:
+                    acc2[hh] = term
+                elif i < 7:
+                    acc2[hh] += term
+                else:
+                    s2b[hh, 2 * g:2 * g + 2] = (acc2[hh] + term).astype(BF16).reshape(2, 64, 256)
         for t in ((4, 5, 1) if g == 0 else (3, 2, 6, 7)):
             send(s2b.at[zs[t] // 4, t % 4], stg.at[z], s3_s.at[t - 1], s3_r.at[t - 1], place(x, y, zs[t], c))
     stg[z] = s2b[zh, 0]
@@ -278,14 +275,11 @@
             prev = st[h, pl.ds(at, 64), :]
             post = st[h, pl.ds(at + 16, 64), :]
             end = v[h] - cx * (post - prev) * 0.5 - cy * (after[h] - before[h]) * 0.5
-            end_v[xr, :, ln] = end.reshape(8, 8, 128)
+            end_out[xr, :, ln] = end.reshape(8, 8, 128)
             m = wei_v[xr, :, ln].reshape(64, 128) * (end - inn_v[xr, :, ln].reshape(64, 128))
             mis[h, pl.ds(at, 64), :] = m
             qx[h, pl.ds(at + 8, 64), :] = cx * m
             py[h, pl.ds(at, 64), :] = cy * m
-
-    store_end = pltpu.make_async_copy(end_v, end_out, loc_sem.at[7])
-    store_end.start()
 
     first, last = fringe(qx)
     edges(lambda h: py[h], hps, hpr, hl, hr, k_s, k_r, first, last)
@@ -341,7 +335,6 @@
         value = share(g, mine)
         for h in range(2):
             pown[h, rows] = value[:, h * 128:(h + 1) * 128]
-    hand(1, 2, pl.ds(0, 256))
 
     def lines(h, q):
         cols = pl.ds(pl.multiple_of(q * 512, 512), 512)
@@ -355,9 +348,11 @@
     for h in range(2):
         for k, rows in ((0, pl.ds(0, 128)), (1, pl.ds(128, 128))) if h == 0 else ((2, pl.ds(0, 256)),):
             arrived(pg.at[h, 0, o, rows], s6_r.at[k, 0, o])
-            for t in range(1, 4):
+            for t in (1, 3, 2):
                 for cc in range(2):
                     arrived(pg.at[h, t, cc, rows], s6_r.at[k, t, cc])
+            if k == 0:
+                hand(1, 2, pl.ds(0, 256))
         pb[h, c] = (three(h, c) + pown[h]).astype(BF16)
         pb[h, o] = (three(h, o) + pg[h, 0, o].astype(F32)).astype(BF16)
         for t in (2, 1, 3):
@@ -398,10 +393,7 @@
             arrived(go.at[h, l], s8_r.at[h, l])
         for l in range(8):
             nat[h, pl.ds(l, 64, stride=8), :] = go[h, l].astype(F32)
-        grad_v[:, :, ln] = ctl_v[:, :, ln].astype(F32) + nat[h].reshape(64, 8, 128)
-    store_grad = pltpu.make_async_copy(grad_v, grad_out, loc_sem.at[8])
-    store_grad.start()
-
+        grad_out[:, :, ln] = ctl_v[:, :, ln].astype(F32) + nat[h].reshape(64, 8, 128)
     for copy in pending:
         copy.wait_send()
 
@@ -410,9 +402,6 @@
         for h in range(2):
             far0[h].wait_send()
             far8[h].wait_send()
-
-    store_end.wait()
-    store_grad.wait()
 
 
 def per_device(control, innovation, obs_weight, courant_x, courant_y, filter_x, filter_y):
@@ -428,15 +417,14 @@
     shares = pltpu.VMEM((2, 4, 2, 256, 128), BF16)
     sums = pltpu.VMEM((2, 3, 512, 128), BF16)
     scratch = [
-        pltpu.VMEM((64, 8, 256), BF16), big, big, big, big, big, big,
+        pltpu.VMEM((64, 8, 256), BF16), big, big, big, big,
         half, levh,
         pltpu.VMEM((2, 32, 64, 128), BF16),
         pltpu.VMEM((2, 4, 4, 16, 2048), BF16),
         pltpu.VMEM((2, 8, 32, 2048), BF16),
-        pltpu.VMEM((512, 128), F32),
-        pltpu.VMEM((2, 2, 256, 128), BF16),
-        pltpu.VMEM((2, 8, 256, 128), BF16),
-        pltpu.VMEM((2, 256, 256), F32),
+        pltpu.VMEM((2, 4, 64, 256), BF16),
+        pltpu.VMEM((8, 256, 256), BF16),
+        pltpu.VMEM((2, 128, 256), F32),
         planes, lev,
         ext, halo, halo, col, col, ext, half, half, half, halo, halo, lev, planes,
         shares,
@@ -446,22 +434,22 @@
         sums,
         pltpu.VMEM((2, 512, 128), F32),
         sums, levh, levh,
-        dma(9), dma(3, 2), dma(3, 2), dma(1), dma(1), dma(2), dma(2), dma(4), dma(4),
+        dma(7), dma(3, 2), dma(3, 2), dma(1), dma(1), dma(2), dma(2), dma(4), dma(4),
         dma(1), dma(1), dma(3), dma(3), dma(4), dma(4),
-        dma(2, 8), dma(2, 8), dma(2, 3, 4), dma(2, 3, 4), dma(3, 4, 2), dma(3, 4, 2), dma(7), dma(7),
+        dma(2, 8), dma(2, 8), dma(2, 3, 4), dma(2, 3, 4), dma(4, 4, 2), dma(4, 4, 2), dma(7), dma(7),
         dma(4), dma(4), dma(4), dma(4), dma(7), dma(7), dma(3, 4, 2), dma(3, 4, 2),
         dma(2, 3), dma(2, 3), dma(2, 4, 2), dma(2, 8),
     ]
-    out = jax.ShapeDtypeStruct((64, 8, 256), F32)
+    out = pltpu.VMEM((64, 8, 256), F32)
     anywhere = pl.BlockSpec(memory_space=pl.ANY)
     return pl.pallas_call(
         kernel,
         out_shape=(out, out),
         in_specs=[anywhere] * 7,
-        out_specs=(anywhere, anywhere),
+        out_specs=(pl.BlockSpec(memory_space=pltpu.VMEM),) * 2,
         scratch_shapes=scratch,
         compiler_params=pltpu.CompilerParams(
-            collective_id=0, has_side_effects=True, vmem_limit_bytes=60 * 1024 * 1024),
+            collective_id=0, has_side_effects=True, vmem_limit_bytes=62 * 1024 * 1024),
         cost_estimate=pl.CostEstimate(flops=2150000000, bytes_accessed=5000000, transcendentals=0),
     )(control, innovation, obs_weight, courant_x, courant_y,
       filter_x.reshape(4, 16, 2048), filter_y.reshape(8, 32, 2048))

time: 108 us -> 103 us (0.954)
  Pallas kernels: 104 us -> 101 us
  local copies, waits for them, and re-layouts: 2.72 us -> 1.59 us
    pallas_call x1, Pallas kernels: 104 us -> 101 us  [per_device(): pl.pallas_call(kernel, out_shape=(out, out), in_specs=[anywhere] * 7, out...]
    unnamed x4 -> x2, local copies, waits for them, and re-layouts: 2.72 us -> 1.59 us
where the time goes in v3:
time: 103 us
  Pallas kernels  101 us (98%)
  local copies, waits for them, and re-layouts  1.59 us (2%)
    pallas_call x1, Pallas kernels, per_device(): pl.pallas_call(kernel, out_shape=(out, out), in_specs=[anywhere] * 7, out...  101 us

profile of v3, /device:TPU:1, one launch (start us, length us, event | category | flops | bytes accessed | tf_op | source)
XLA Modules:
  0.0 103.0 jit_solution(15075416811007320477)
XLA Ops:
  0.6 100.8 %shard_map.86 = (f32[64,8,256]{2,1,0:T(8,128)S(1)}, f32[64,8,256]{2,1,0:T(8,128)S(1)}) custom-call(bf16[64,8,256]{2,1,0:T(8,128)(2,1)} %ctl.1, f32[64,8,256]{2,1,0:T(8,128)} %innov.1, f32[64,8,256]{2,1,0:T(8,128)} %weight.1, f32[64,8,256]{2,1,0:T(8,128)} %cou_x.1, f32[64,8,256]{2,1,0:T(8,128)} %cou_y.1, bf16[4,16,2048]{2,1,0:T(8,128)(2,1)} %bitcast.3, ...), custom_call_target="tpu_custom_call" | custom-call | flops 2150000128 | bytes 5000000 | tf_op jit(solution)/shard_map/pallas_call | solution.py:445
  101.4 0.8 copy.11
  102.2 0.8 copy.12

commit v4 on v3

--- a/solution.py
+++ b/solution.py
@@ -17,12 +17,12 @@
     end_out, grad_out,
     ctl_v, inn_v, wei_v, cx_v, cy_v,
     nat, snd0, cg, fxb, fyb, s1b, s1g, acc2, s2b, stg,
-    st, hys, hyr, hl, hr, qx, py, mis, adj, hps, hpr, ags, ag,
+    st, hys, hyr, cor, frow, fcs, fcr, hl, hr, ql, qr, qx, py, mis, adj, ags, ag,
     psend, pown, pg, pb, gsend, gown, gg, gs, go,
     loc_sem, f1_s, f1_r, fo_s, fo_r, f2_s, f2_r, fr_s, fr_r,
     g1_s, g1_r, g2_s, g2_r, gr_s, gr_r,
     s0_s, s0_r, s1_s, s1_r, s2_s, s2_r, s3_s, s3_r,
-    h_s, h_r, k_s, k_r, s5_s, s5_r, s6_s, s6_r, s7_s, s7_r, s8_s, s8_r,
+    h_s, h_r, fw_s, fw_r, fc_s, fc_r, s5_s, s5_r, s6_s, s6_r, s7_s, s7_r, s8_s, s8_r,
 ):
     gx = lax.axis_index("gx")
     gy = lax.axis_index("gy")
@@ -54,6 +54,7 @@
     down = (lax.rem(gx + 31, 32), gy)
     right = (gx, lax.rem(gy + 1, 8))
     left = (gx, lax.rem(gy + 7, 8))
+    corners = [(up[0], right[1]), (up[0], left[1]), (down[0], right[1]), (down[0], left[1])]
 
     load_ctl = pltpu.make_async_copy(ctl, ctl_v, loc_sem.at[0])
     load_ctl.start()
@@ -73,7 +74,7 @@
     for t in range(1, 4):
         partners += [place(xs[t], y, z, c), place(xs[t], y, z, o)]
         partners += [place(x, ys[t], z, c)]
-    partners += [up, down, left, right]
+    partners += [up, down, left, right] + corners
     for dev in partners:
         pl.semaphore_signal(barrier, inc=1, device_id=dev, device_id_type=MESH)
 
@@ -150,6 +151,15 @@
                      s2_s.at[d, t, r], s2_r.at[d, t, c], place(xs[t], y, z, r))
         send(s1b.at[o, d], s1g.at[mine, rows], s2_s.at[d, 0, 0], s2_r.at[d, 0, 0], sib)
         s1g[mine, rows] = s1b[c, d]
+
+    for f, (field, held) in enumerate(((innov, inn_v), (weight, wei_v), (cou_x, cx_v), (cou_y, cy_v))):
+        loads[2 + f].wait()
+        send(field.at[0], frow.at[f, 1], fw_s.at[f, 0], fw_r.at[f, 1], down)
+        send(field.at[63], frow.at[f, 0], fw_s.at[f, 1], fw_r.at[f, 0], up)
+        fcs[0, f:f + 1, :] = held[:, :, 0:128].reshape(512, 128).T[0:1]
+        fcs[1, f:f + 1, :] = held[:, :, 128:256].reshape(512, 128).T[127:128]
+    send(fcs.at[0], fcr.at[0], fc_s.at[0], fc_r.at[0], left)
+    send(fcs.at[1], fcr.at[1], fc_s.at[1], fc_r.at[1], right)
 
     for h in range(2):
         for t in (3, 1, 2):
@@ -210,70 +220,102 @@
     def spread(l):
         value = stg[l].astype(F32)
         for h in range(2):
-            st[h, pl.ds(8 + l, 64, stride=8), :] = value[:, h * 128:(h + 1) * 128]
+            st[h, pl.ds(16 + l, 64, stride=8), :] = value[:, h * 128:(h + 1) * 128]
 
     for t in range(1, 8):
         arrived(stg.at[lax.rem(z + 8 - t, 8)], s3_r.at[t - 1])
     for l in range(8):
         spread(l)
 
-    def edges(field, hsend, hrecv, hleft, hright, ssem, rsem, ref_first, ref_last):
-        send(ref_first(0), ref_last(1), ssem.at[0], rsem.at[0], down)
-        send(ref_last(0), ref_first(1), ssem.at[1], rsem.at[1], up)
-        hsend[0] = field(0).T[0:8]
-        send(hsend.at[0], hrecv.at[0], ssem.at[2], rsem.at[2], left)
-        hsend[1] = field(1).T[120:128]
-        send(hsend.at[1], hrecv.at[1], ssem.at[3], rsem.at[3], right)
-        arrived(ref_last(1), rsem.at[0])
-        arrived(ref_first(1), rsem.at[1])
-        arrived(hrecv.at[0], rsem.at[2])
-        arrived(hrecv.at[1], rsem.at[3])
-        keep_r = jnp.where(gy == 7, 0.0, 1.0).astype(F32)
-        keep_l = jnp.where(gy == 0, 0.0, 1.0).astype(F32)
-        hright[...] = jnp.broadcast_to(hrecv[0, 0:1, :] * keep_r, (128, 512)).T
-        hleft[...] = jnp.broadcast_to(hrecv[1, 7:8, :] * keep_l, (128, 512)).T
-
-    def fringe(ref):
-        first = lambda k: ref.at[:, pl.ds(8, 8)] if k == 0 else ref.at[:, pl.ds(0, 8)]
-        last = lambda k: ref.at[:, pl.ds(512, 8)] if k == 0 else ref.at[:, pl.ds(520, 8)]
-        return first, last
-
-    def clear(ref):
-        @pl.when(gx == 0)
-        def _():
-            ref[:, 0:8, :] = jnp.zeros((2, 8, 128), F32)
-
-        @pl.when(gx == 31)
-        def _():
-            ref[:, 520:528, :] = jnp.zeros((2, 8, 128), F32)
-
-    first, last = fringe(st)
-    edges(lambda h: st[h, 8:520, :], hys, hyr, hl, hr, h_s, h_r, first, last)
-    clear(st)
-    for load in loads[2:]:
-        load.wait()
-
-    lane = lax.broadcasted_iota(jnp.int32, (64, 128), 1)
+    send(st.at[:, pl.ds(16, 16)], st.at[:, pl.ds(528, 16)], h_s.at[0], h_r.at[0], down)
+    send(st.at[:, pl.ds(512, 16)], st.at[:, pl.ds(0, 16)], h_s.at[1], h_r.at[1], up)
+    for k, (h, at) in enumerate(((1, 520), (0, 520), (1, 16), (0, 16))):
+        send(st.at[h, pl.ds(at, 8)], cor.at[k], h_s.at[4 + k], h_r.at[4 + k], corners[k])
+    hys[0] = st[0, 16:528, :].T[0:8]
+    send(hys.at[0], hyr.at[0], h_s.at[2], h_r.at[2], left)
+    hys[1] = st[1, 16:528, :].T[120:128]
+    send(hys.at[1], hyr.at[1], h_s.at[3], h_r.at[3], right)
+    for f in range(4):
+        for k in range(2):
+            arrived(frow.at[f, k], fw_r.at[f, k])
+    for k in range(2):
+        arrived(fcr.at[k], fc_r.at[k])
+    arrived(st.at[:, pl.ds(528, 16)], h_r.at[0])
+    arrived(st.at[:, pl.ds(0, 16)], h_r.at[1])
+    for k in range(2):
+        arrived(hyr.at[k], h_r.at[2 + k])
+    for k in range(4):
+        arrived(cor.at[k], h_r.at[4 + k])
+
+    @pl.when(gx == 0)
+    def _():
+        st[:, 0:16, :] = jnp.zeros((2, 16, 128), F32)
+
+    @pl.when(gx == 31)
+    def _():
+        st[:, 528:544, :] = jnp.zeros((2, 16, 128), F32)
+
+    keep_u = jnp.where(gx == 0, 0.0, 1.0).astype(F32)
+    keep_d = jnp.where(gx == 31, 0.0, 1.0).astype(F32)
+    keep_l = jnp.where(gy == 0, 0.0, 1.0).astype(F32)
+    keep_r = jnp.where(gy == 7, 0.0, 1.0).astype(F32)
+    cor[0] = cor[0] * (keep_u * keep_l)
+    cor[1] = cor[1] * (keep_u * keep_r)
+    cor[2] = cor[2] * (keep_d * keep_l)
+    cor[3] = cor[3] * (keep_d * keep_r)
+    beyond_l = hyr[1, 6:8, :] * keep_l
+    beyond_r = hyr[0, 0:2, :] * keep_r
+    hr[...] = jnp.broadcast_to(beyond_r[0:1], (128, 512)).T
+    hl[...] = jnp.broadcast_to(beyond_l[1:2], (128, 512)).T
 
     def beside(v0, v1, left_halo, right_halo):
+        lane = lax.broadcasted_iota(jnp.int32, v0.shape, 1)
         f0, f1 = pltpu.roll(v0, 127, 1), pltpu.roll(v1, 127, 1)
         b0, b1 = pltpu.roll(v0, 1, 1), pltpu.roll(v1, 1, 1)
         after = (jnp.where(lane == 127, f1, f0), jnp.where(lane == 127, right_halo, f1))
         before = (jnp.where(lane == 0, left_halo, b0), jnp.where(lane == 0, b0, b1))
         return before, after
 
+    for k, at, to, keep in ((0, 8, 0, keep_u), (1, 528, 520, keep_d)):
+        v = [st[h, at:at + 8, :] for h in range(2)]
+        before, after = beside(v[0], v[1], pltpu.roll(cor[2 * k], 1, 1), pltpu.roll(cor[2 * k + 1], 127, 1))
+        for h in range(2):
+            ln = slice(h * 128, (h + 1) * 128)
+            cx, cy = frow[2, k, :, ln], frow[3, k, :, ln]
+            end = (v[h] - cx * (st[h, at + 8:at + 16, :] - st[h, at - 8:at, :]) * 0.5
+                   - cy * (after[h] - before[h]) * 0.5)
+            qx[h, to:to + 8, :] = keep * cx * (frow[1, k, :, ln] * (end - frow[0, k, :, ln]))
+
+    spot = lax.broadcasted_iota(jnp.int32, (8, 512), 1)
+    level = lax.broadcasted_iota(jnp.int32, (8, 512), 0)
+    ahead = lax.broadcasted_iota(jnp.int32, (1, 512), 1)
+
+    def along(k, at):
+        column = jnp.broadcast_to(cor[k][:, at:at + 1], (8, 512))
+        return jnp.sum(jnp.where(lax.rem(spot, 8) == level, column, 0.0), axis=0, keepdims=True)
+
+    def flux(k, value, low, high, first, last, keep):
+        prev = jnp.where(ahead < 8, first, pltpu.roll(value, 8, 1))
+        post = jnp.where(ahead >= 504, last, pltpu.roll(value, 504, 1))
+        inn, wei, cx, cy = [fcr[k, f:f + 1, :] for f in range(4)]
+        end = value - cx * (post - prev) * 0.5 - cy * (high - low) * 0.5
+        return jnp.broadcast_to(keep * cy * (wei * (end - inn)), (128, 512)).T
+
+    ql[...] = flux(1, beyond_l[1:2], beyond_l[0:1], hys[0, 0:1, :], along(0, 127), along(2, 127), keep_l)
+    qr[...] = flux(0, beyond_r[0:1], hys[1, 7:8, :], beyond_r[1:2], along(1, 0), along(3, 0), keep_r)
+
     @pl.loop(0, 8)
     def _(i):
         at = pl.multiple_of(i * 64, 64)
         xr = pl.ds(i * 8, 8)
-        v = [st[h, pl.ds(at + 8, 64), :] for h in range(2)]
+        v = [st[h, pl.ds(at + 16, 64), :] for h in range(2)]
         before, after = beside(v[0], v[1], hl[pl.ds(at, 64), :], hr[pl.ds(at, 64), :])
         for h in range(2):
             ln = slice(h * 128, (h + 1) * 128)
             cx = cx_v[xr, :, ln].reshape(64, 128)
             cy = cy_v[xr, :, ln].reshape(64, 128)
-            prev = st[h, pl.ds(at, 64), :]
-            post = st[h, pl.ds(at + 16, 64), :]
+            prev = st[h, pl.ds(at + 8, 64), :]
+            post = st[h, pl.ds(at + 24, 64), :]
             end = v[h] - cx * (post - prev) * 0.5 - cy * (after[h] - before[h]) * 0.5
             end_out[xr, :, ln] = end.reshape(8, 8, 128)
             m = wei_v[xr, :, ln].reshape(64, 128) * (end - inn_v[xr, :, ln].reshape(64, 128))
@@ -281,15 +323,11 @@
             qx[h, pl.ds(at + 8, 64), :] = cx * m
             py[h, pl.ds(at, 64), :] = cy * m
 
-    first, last = fringe(qx)
-    edges(lambda h: py[h], hps, hpr, hl, hr, k_s, k_r, first, last)
-    clear(qx)
-
     @pl.loop(0, 8)
     def _(i):
         at = pl.multiple_of(i * 64, 64)
         v = [py[h, pl.ds(at, 64), :] for h in range(2)]
-        before, after = beside(v[0], v[1], hl[pl.ds(at, 64), :], hr[pl.ds(at, 64), :])
+        before, after = beside(v[0], v[1], ql[pl.ds(at, 64), :], qr[pl.ds(at, 64), :])
         for h in range(2):
             prev = qx[h, pl.ds(at, 64), :]
             post = qx[h, pl.ds(at + 16, 64), :]
@@ -426,7 +464,10 @@
         pltpu.VMEM((8, 256, 256), BF16),
         pltpu.VMEM((2, 128, 256), F32),
         planes, lev,
-        ext, halo, halo, col, col, ext, half, half, half, halo, halo, lev, planes,
+        pltpu.VMEM((2, 544, 128), F32), halo, halo,
+        pltpu.VMEM((4, 8, 128), F32),
+        pltpu.VMEM((4, 2, 8, 256), F32), halo, halo,
+        col, col, col, col, ext, half, half, half, lev, planes,
         shares,
         pltpu.VMEM((2, 256, 128), F32),
         shares,
@@ -437,7 +478,7 @@
         dma(7), dma(3, 2), dma(3, 2), dma(1), dma(1), dma(2), dma(2), dma(4), dma(4),
         dma(1), dma(1), dma(3), dma(3), dma(4), dma(4),
         dma(2, 8), dma(2, 8), dma(2, 3, 4), dma(2, 3, 4), dma(4, 4, 2), dma(4, 4, 2), dma(7), dma(7),
-        dma(4), dma(4), dma(4), dma(4), dma(7), dma(7), dma(3, 4, 2), dma(3, 4, 2),
+        dma(8), dma(8), dma(4, 2), dma(4, 2), dma(2), dma(2), dma(7), dma(7), dma(3, 4, 2), dma(3, 4, 2),
         dma(2, 3), dma(2, 3), dma(2, 4, 2), dma(2, 8),
     ]
     out = pltpu.VMEM((64, 8, 256), F32)

time: 103 us -> 101 us (0.981)
  Pallas kernels: 101 us -> 98.4 us
    pallas_call x1, Pallas kernels: 101 us -> 98.4 us  [per_device(): pl.pallas_call(kernel, out_shape=(out, out), in_specs=[anywhere] * 7, out...]
where the time goes in v4:
time: 101 us
  Pallas kernels  98.4 us (97%)
  local copies, waits for them, and re-layouts  1.59 us (2%)
    pallas_call x1, Pallas kernels, per_device(): pl.pallas_call(kernel, out_shape=(out, out), in_specs=[anywhere] * 7, out...  98.4 us

profile of v4, /device:TPU:1, one launch (start us, length us, event | category | flops | bytes accessed | tf_op | source)
XLA Modules:
  0.0 100.6 jit_solution(5812389258435560955)
XLA Ops:
  0.6 98.4 %shard_map.86 = (f32[64,8,256]{2,1,0:T(8,128)S(1)}, f32[64,8,256]{2,1,0:T(8,128)S(1)}) custom-call(bf16[64,8,256]{2,1,0:T(8,128)(2,1)} %ctl.1, f32[64,8,256]{2,1,0:T(8,128)} %innov.1, f32[64,8,256]{2,1,0:T(8,128)} %weight.1, f32[64,8,256]{2,1,0:T(8,128)} %cou_x.1, f32[64,8,256]{2,1,0:T(8,128)} %cou_y.1, bf16[4,16,2048]{2,1,0:T(8,128)(2,1)} %bitcast.3, ...), custom_call_target="tpu_custom_call" | custom-call | flops 2150000128 | bytes 5000000 | tf_op jit(solution)/shard_map/pallas_call | solution.py:486
  99.0 0.8 copy.11
  99.8 0.8 copy.12

commit v5 on v4

--- a/solution.py
+++ b/solution.py
@@ -8,6 +8,9 @@
 MESH = pl.DeviceIdType.MESH
 F32 = jnp.float32
 BF16 = jnp.bfloat16
+F_ONE = ((2, 2, pl.ds(0, 1024)), (2, 6, pl.ds(1024, 1024)), (1, 7, pl.ds(0, 2048)), (3, 1, pl.ds(0, 2048)))
+
+
 def place(x, y, z, c):
     return (y * 8 + lax.rem(z, 4) * 2 + c, (z // 4) * 4 + x)
 
@@ -88,69 +91,30 @@
     pl.semaphore_wait(barrier, len(partners))
 
     slot0 = zl * 2 + c
+    x2 = xs[2]
+    own0, far0 = [], []
     for h in range(2):
         for t in (4, 3, 5, 2, 6, 1, 7):
             send(snd0.at[h, zs[t]], cg.at[h, gx], s0_s.at[h, t], s0_r.at[h, slot0], place(x, y, zs[t], zh))
-    own0 = [pltpu.make_async_copy(snd0.at[h, z], cg.at[h, gx], s0_r.at[h, slot0]) for h in range(2)]
-    far0 = [pltpu.make_async_remote_copy(
-        src_ref=snd0.at[h, z], dst_ref=cg.at[h, gx], send_sem=s0_s.at[h, 0], recv_sem=s0_r.at[h, slot0],
-        device_id=sib, device_id_type=MESH) for h in range(2)]
-
-    @pl.when(zh == c)
-    def _():
-        own0[0].start()
-        own0[1].start()
-
-    @pl.when(zh != c)
-    def _():
-        far0[0].start()
-        far0[1].start()
+        src, dst = snd0.at[h, z], cg.at[h, gx]
+        own0.append(pltpu.make_async_copy(src, dst, s0_r.at[h, slot0]))
+        far0.append(pltpu.make_async_remote_copy(
+            src_ref=src, dst_ref=dst, send_sem=s0_s.at[h, 0], recv_sem=s0_r.at[h, slot0],
+            device_id=sib, device_id_type=MESH))
+
+        @pl.when(zh == c)
+        def _():
+            own0[h].start()
+
+        @pl.when(zh != c)
+        def _():
+            far0[h].start()
+
+        q = x2 if h else x
+        for k, (d, dz, cols) in enumerate(F_ONE):
+            send(fx.at[q, :, cols], fxb.at[c, d, q, :, cols], f1_s.at[k, h], f1_r.at[k, h], place(x, y, zs[dz], c))
 
     send(fx, fxb.at[c, 0], fo_s.at[0], fo_r.at[0], sib)
-
-    def ring(h):
-        for s in range(4):
-            for cc in range(2):
-                arrived(cg.at[h, y * 8 + 2 * s + cc], s0_r.at[h, 2 * s + cc])
-            block = cg.at[h, pl.ds(y * 8 + 2 * s, 2)]
-            for t in (2, 1, 3):
-                send(block, block, s1_s.at[h, t - 1, s], s1_r.at[h, t - 1, s], place(x, ys[t], z, c))
-
-    ring(0)
-
-    x2 = xs[2]
-    for d, k, q, dz in ((2, 0, x, 6), (1, 0, x, 7), (3, 0, x, 1), (2, 1, x2, 2), (1, 1, x2, 7), (3, 1, x2, 1)):
-        send(fx.at[q], fxb.at[c, d, q], f1_s.at[d - 1, k], f1_r.at[d - 1, k], place(x, y, zs[dz], c))
-
-    ring(1)
-
-    for d in range(1, 4):
-        arrived(fxb.at[c, d, x], f1_r.at[d - 1, 0])
-    quarter = fxb.at[c, pl.ds(1, 3), x]
-    for t in (1, 3):
-        send(quarter, quarter, f2_s.at[t // 2], f2_r.at[t // 2], place(xs[t], y, z, c))
-    send(quarter, quarter, fr_s.at[0], fr_r.at[0], sib)
-    for d in range(1, 4):
-        arrived(fxb.at[c, d, x2], f1_r.at[d - 1, 1])
-    quarter = fxb.at[c, pl.ds(1, 3), x2]
-    send(quarter, quarter, fr_s.at[2], fr_r.at[2], sib)
-
-    send(fy.at[e], fyb.at[zh, e], g1_s.at[0], g1_r.at[0], place(x, y, zs[4], c))
-
-    mine = c * 4 + x
-
-    def smooth(d):
-        a = fxb[:, d].reshape(128, 2048)
-        for h in range(2):
-            v = jnp.dot(a, cg[h].reshape(2048, 128), preferred_element_type=F32)
-            s1b[:, d, :, h * 128:(h + 1) * 128] = v.astype(BF16).reshape(2, 64, 128)
-        rows = pl.ds(d * 64, 64)
-        for t in (2, 1, 3):
-            for r in range(2):
-                send(s1b.at[r, d], s1g.at[mine, rows],
-                     s2_s.at[d, t, r], s2_r.at[d, t, c], place(xs[t], y, z, r))
-        send(s1b.at[o, d], s1g.at[mine, rows], s2_s.at[d, 0, 0], s2_r.at[d, 0, 0], sib)
-        s1g[mine, rows] = s1b[c, d]
 
     for f, (field, held) in enumerate(((innov, inn_v), (weight, wei_v), (cou_x, cx_v), (cou_y, cy_v))):
         loads[2 + f].wait()
@@ -161,69 +125,111 @@
     send(fcs.at[0], fcr.at[0], fc_s.at[0], fc_r.at[0], left)
     send(fcs.at[1], fcr.at[1], fc_s.at[1], fc_r.at[1], right)
 
+    def ring(h):
+        for s in range(4):
+            for cc in range(2):
+                arrived(cg.at[h, y * 8 + 2 * s + cc], s0_r.at[h, 2 * s + cc])
+            block = cg.at[h, pl.ds(y * 8 + 2 * s, 2)]
+            for t in (2, 1, 3):
+                send(block, block, s1_s.at[h, t - 1, s], s1_r.at[h, t - 1, s], place(x, ys[t], z, c))
+
+    ring(0)
+
+    send(fy.at[e], fyb.at[zh, e], g1_s.at[0], g1_r.at[0], place(x, y, zs[4], c))
+
+    for k, (d, dz, cols) in enumerate(F_ONE):
+        arrived(fxb.at[c, d, x, :, cols], f1_r.at[k, 0])
+    quarter = fxb.at[c, pl.ds(1, 3), x]
+    for t in (1, 3):
+        send(quarter, quarter, f2_s.at[t // 2], f2_r.at[t // 2], place(xs[t], y, z, c))
+    send(quarter, quarter, fr_s.at[0], fr_r.at[0], sib)
+
+    ring(1)
+
+    for k, (d, dz, cols) in enumerate(F_ONE):
+        arrived(fxb.at[c, d, x2, :, cols], f1_r.at[k, 1])
+    quarter = fxb.at[c, pl.ds(1, 3), x2]
+    send(quarter, quarter, fr_s.at[2], fr_r.at[2], sib)
+
+    for t in (1, 3):
+        part = fxb.at[c, pl.ds(1, 3), xs[4 - t]]
+        arrived(part, f2_r.at[t // 2])
+        send(part, part, fr_s.at[t], fr_r.at[t], sib)
+
+    loads[0].wait()
+    loads[1].wait()
+    arrived(fxb.at[o, 0], fo_r.at[0])
+    for t in range(4):
+        arrived(fxb.at[o, pl.ds(1, 3), xs[(4 - t) % 4]], fr_r.at[t])
+
+    mine = c * 4 + x
+    zo = 1 - zh
     for h in range(2):
         for t in (3, 1, 2):
             for s in range(4):
                 arrived(cg.at[h, pl.ds(ys[4 - t] * 8 + 2 * s, 2)], s1_r.at[h, t - 1, s])
-    loads[0].wait()
-    loads[1].wait()
-    arrived(fxb.at[o, 0], fo_r.at[0])
-    smooth(0)
-    for t in (1, 3):
-        part = fxb.at[c, pl.ds(1, 3), xs[4 - t]]
-        arrived(part, f2_r.at[t // 2])
-        send(part, part, fr_s.at[t], fr_r.at[t], sib)
-    for t in range(4):
-        arrived(fxb.at[o, pl.ds(1, 3), xs[(4 - t) % 4]], fr_r.at[t])
-    smooth(1)
-    smooth(2)
-    smooth(3)
-
-    zo = 1 - zh
-    arrived(fyb.at[zo, e], g1_r.at[0])
-    for t in (2, 1, 3):
-        send(fyb.at[zo, e], fyb.at[zo, e], g2_s.at[t - 1], g2_r.at[t - 1], place(x, ys[t], z, c))
-    send(fyb.at[zo, e], fyb.at[zo, e], gr_s.at[0], gr_r.at[0], sib)
-
-    def cols_dot(q, hh, g):
-        cols = pl.ds(pl.multiple_of(q * 256, 256), 256)
-        b = fyb[hh, :, :, cols].reshape(256, 256)
-        a = s1g[q, g * 128:(g + 1) * 128, :]
+        for g in range(2):
+            k = 2 * h + g
+            rows = pl.ds(g * 128, 128)
+            a = fxb[:, 2 * g:2 * g + 2].reshape(256, 2048)
+            v = jnp.dot(a, cg[h].reshape(2048, 128), preferred_element_type=F32)
+            s1b[h, :, rows] = v.astype(BF16).reshape(2, 128, 128)
+            for t in (2, 1, 3):
+                for r in range(2):
+                    send(s1b.at[h, r, rows], s1g.at[h, mine, rows],
+                         s2_s.at[k, t, r], s2_r.at[k, t, c], place(xs[t], y, z, r))
+            send(s1b.at[h, o, rows], s1g.at[h, mine, rows], s2_s.at[k, 0, 0], s2_r.at[k, 0, 0], sib)
+        s1g[h, mine] = s1b[h, c]
+        if h == 0:
+            arrived(fyb.at[zo, e], g1_r.at[0])
+            for t in (2, 1, 3):
+                send(fyb.at[zo, e], fyb.at[zo, e], g2_s.at[t - 1], g2_r.at[t - 1], place(x, ys[t], z, c))
+            send(fyb.at[zo, e], fyb.at[zo, e], gr_s.at[0], gr_r.at[0], sib)
+
+    def cols_dot(h, q, hh, g):
+        cols = pl.ds(pl.multiple_of(q * 256 + h * 128, 128), 128)
+        b = fyb[hh, :, :, cols].reshape(256, 128)
+        a = s1g[h, q, g * 128:(g + 1) * 128, :]
         return lax.dot_general(a, b, (((1,), (1,)), ((), ())), preferred_element_type=F32)
+
+    sources = [(0, 0, mine), (0, 0, o * 4 + x)]
+    sources += [(t, cc, cc * 4 + xs[4 - t]) for t in (3, 1, 2) for cc in range(2)]
+
+    def level_up(k, hh):
+        for h in range(2):
+            for g in range(2):
+                rows = pl.ds(g * 128, 128)
+                for i, (t, cc, q) in enumerate(sources):
+                    if i and k == 0:
+                        arrived(s1g.at[h, q, rows], s2_r.at[2 * h + g, t, cc])
+                    term = cols_dot(h, q, hh, g)
+                    acc2[g] = acc2[g] + term if h or i else term
+                if h:
+                    s2b[hh, 2 * g:2 * g + 2] = acc2[g].astype(BF16).reshape(2, 64, 256)
+                    for d in ((1, 0) if g == 0 else (2, 3)):
+                        if k or d:
+                            send(s2b.at[hh, d], stg.at[z], s3_s.at[k * 4 + d], s3_r.at[k * 4 + d],
+                                 place(x, y, hh * 4 + lax.rem(zl + d, 4), c))
 
     for t in (3, 1, 2):
         eq = ys[4 - t] * 2 + c
         arrived(fyb.at[zo, eq], g2_r.at[t - 1])
         send(fyb.at[zo, eq], fyb.at[zo, eq], gr_s.at[t], gr_r.at[t], sib)
+    level_up(0, zh)
+    stg[z] = s2b[zh, 0]
     for t in range(4):
         arrived(fyb.at[zo, ys[(4 - t) % 4] * 2 + o], gr_r.at[t])
-    sources = [(0, 0, mine), (0, 0, o * 4 + x)]
-    sources += [(t, cc, cc * 4 + xs[4 - t]) for t in (3, 1, 2) for cc in range(2)]
-
-    for g in range(2):
-        for i, (t, cc, q) in enumerate(sources):
-            if i:
-                for d in (2 * g, 2 * g + 1):
-                    arrived(s1g.at[q, pl.ds(d * 64, 64)], s2_r.at[d, t, cc])
-            for hh in range(2):
-                term = cols_dot(q, hh, g)
-                if i == 0:
-                    acc2[hh] = term
-                elif i < 7:
-                    acc2[hh] += term
-                else:
-                    s2b[hh, 2 * g:2 * g + 2] = (acc2[hh] + term).astype(BF16).reshape(2, 64, 256)
-        for t in ((4, 5, 1) if g == 0 else (3, 2, 6, 7)):
-            send(s2b.at[zs[t] // 4, t % 4], stg.at[z], s3_s.at[t - 1], s3_r.at[t - 1], place(x, y, zs[t], c))
-    stg[z] = s2b[zh, 0]
+    level_up(1, zo)
 
     def spread(l):
         value = stg[l].astype(F32)
         for h in range(2):
             st[h, pl.ds(16 + l, 64, stride=8), :] = value[:, h * 128:(h + 1) * 128]
 
-    for t in range(1, 8):
-        arrived(stg.at[lax.rem(z + 8 - t, 8)], s3_r.at[t - 1])
+    for k, hh in ((0, zh), (1, zo)):
+        for d in range(4):
+            if k or d:
+                arrived(stg.at[hh * 4 + lax.rem(zl + 4 - d, 4)], s3_r.at[k * 4 + d])
     for l in range(8):
         spread(l)
 
@@ -460,8 +466,8 @@
         pltpu.VMEM((2, 32, 64, 128), BF16),
         pltpu.VMEM((2, 4, 4, 16, 2048), BF16),
         pltpu.VMEM((2, 8, 32, 2048), BF16),
-        pltpu.VMEM((2, 4, 64, 256), BF16),
-        pltpu.VMEM((8, 256, 256), BF16),
+        pltpu.VMEM((2, 2, 256, 128), BF16),
+        pltpu.VMEM((2, 8, 256, 128), BF16),
         pltpu.VMEM((2, 128, 256), F32),
         planes, lev,
         pltpu.VMEM((2, 544, 128), F32), halo, halo,
@@ -475,9 +481,9 @@
         sums,
         pltpu.VMEM((2, 512, 128), F32),
         sums, levh, levh,
-        dma(7), dma(3, 2), dma(3, 2), dma(1), dma(1), dma(2), dma(2), dma(4), dma(4),
+        dma(7), dma(4, 2), dma(4, 2), dma(1), dma(1), dma(2), dma(2), dma(4), dma(4),
         dma(1), dma(1), dma(3), dma(3), dma(4), dma(4),
-        dma(2, 8), dma(2, 8), dma(2, 3, 4), dma(2, 3, 4), dma(4, 4, 2), dma(4, 4, 2), dma(7), dma(7),
+        dma(2, 8), dma(2, 8), dma(2, 3, 4), dma(2, 3, 4), dma(4, 4, 2), dma(4, 4, 2), dma(8), dma(8),
         dma(8), dma(8), dma(4, 2), dma(4, 2), dma(2), dma(2), dma(7), dma(7), dma(3, 4, 2), dma(3, 4, 2),
         dma(2, 3), dma(2, 3), dma(2, 4, 2), dma(2, 8),
     ]

time: 101 us -> 98.8 us (0.978)
  Pallas kernels: 98.4 us -> 96.5 us
    pallas_call x1, Pallas kernels: 98.4 us -> 96.5 us  [per_device(): pl.pallas_call(kernel, out_shape=(out, out), in_specs=[anywhere] * 7, out...]
where the time goes in v5:
time: 98.8 us; the launch traced here: 98.7 us
  Pallas kernels  96.5 us (98%)
  local copies, waits for them, and re-layouts  1.59 us (2%)
    pallas_call x1, Pallas kernels, per_device(): pl.pallas_call(kernel, out_shape=(out, out), in_specs=[anywhere] * 7, out...  96.5 us

profile of v5, /device:TPU:1, one launch (start us, length us, event | category | flops | bytes accessed | tf_op | source)
XLA Modules:
  0.0 98.7 jit_solution(14779092224199719413)
XLA Ops:
  0.6 96.5 %shard_map.86 = (f32[64,8,256]{2,1,0:T(8,128)S(1)}, f32[64,8,256]{2,1,0:T(8,128)S(1)}) custom-call(bf16[64,8,256]{2,1,0:T(8,128)(2,1)} %ctl.1, f32[64,8,256]{2,1,0:T(8,128)} %innov.1, f32[64,8,256]{2,1,0:T(8,128)} %weight.1, f32[64,8,256]{2,1,0:T(8,128)} %cou_x.1, f32[64,8,256]{2,1,0:T(8,128)} %cou_y.1, bf16[4,16,2048]{2,1,0:T(8,128)(2,1)} %bitcast.3, ...), custom_call_target="tpu_custom_call" | custom-call | flops 2150000128 | bytes 5000000 | tf_op jit(solution)/shard_map/pallas_call | solution.py:492
  97.1 0.8 copy.11
  97.9 0.8 copy.12

commit v6 on v5

--- a/solution.py
+++ b/solution.py
@@ -380,9 +380,9 @@
         for h in range(2):
             pown[h, rows] = value[:, h * 128:(h + 1) * 128]
 
-    def lines(h, q):
-        cols = pl.ds(pl.multiple_of(q * 512, 512), 512)
-        a = fxb[:, :, :, :, cols].reshape(512, 512)
+    def lines(h, q, part):
+        cols = pl.ds(pl.multiple_of(q * 512 + part * 256, 256), 256)
+        a = fxb[:, :, :, :, cols].reshape(512, 256)
         b = pb[h].reshape(512, 128)
         return lax.dot_general(a, b, (((0,), (0,)), ((), ())), preferred_element_type=F32)
 
@@ -399,37 +399,36 @@
                 hand(1, 2, pl.ds(0, 256))
         pb[h, c] = (three(h, c) + pown[h]).astype(BF16)
         pb[h, o] = (three(h, o) + pg[h, 0, o].astype(F32)).astype(BF16)
-        for t in (2, 1, 3):
-            gsend[h, t - 1] = lines(h, ys[t]).astype(BF16)
-            send(gsend.at[h, t - 1], gg.at[h, t - 1], s7_s.at[h, t - 1], s7_r.at[h, t - 1], place(x, ys[t], z, c))
-        gown[h] = lines(h, y)
-
-    own8, far8 = [], []
+        for part in range(2):
+            rows = pl.ds(part * 256, 256)
+            for t in (2, 1, 3):
+                gsend[h, t - 1, rows] = lines(h, ys[t], part).astype(BF16)
+                send(gsend.at[h, t - 1, rows], gg.at[h, t - 1, rows],
+                     s7_s.at[h, part, t - 1], s7_r.at[h, part, t - 1], place(x, ys[t], z, c))
+        for part in range(2):
+            gown[h, pl.ds(part * 256, 256)] = lines(h, y, part)
+
+    far8 = []
     for h in range(2):
-        for t in range(1, 4):
-            arrived(gg.at[h, t - 1], s7_r.at[h, t - 1])
-        total = gown[h] + gg[h, 0].astype(F32) + gg[h, 1].astype(F32) + gg[h, 2].astype(F32)
-        gs[h] = total.astype(BF16).reshape(8, 64, 128)
-        for u in (2, 1, 3, 0):
-            zq = lax.rem(zl + u, 4)
-            for v in range(2):
-                cq = o if v else c
-                if u or v:
-                    send(gs.at[h, zq * 2 + cq], go.at[h, z], s8_s.at[h, u, v], s8_r.at[h, z],
-                         place(x, y, c * 4 + zq, cq))
-        src, dst = gs.at[h, zl * 2 + c], go.at[h, z]
-        own8.append(pltpu.make_async_copy(src, dst, s8_r.at[h, z]))
-        far8.append(pltpu.make_async_remote_copy(
-            src_ref=src, dst_ref=dst, send_sem=s8_s.at[h, 0, 0], recv_sem=s8_r.at[h, z],
-            device_id=place(x, y, c * 4 + zl, c), device_id_type=MESH))
-
-        @pl.when(zh == c)
-        def _():
-            own8[h].start()
-
-        @pl.when(zh != c)
-        def _():
-            far8[h].start()
+        for part in range(2):
+            rows = pl.ds(part * 256, 256)
+            total = gown[h, rows]
+            for t in (1, 3, 2):
+                arrived(gg.at[h, t - 1, rows], s7_r.at[h, part, t - 1])
+                total += gg[h, t - 1, rows].astype(F32)
+            gs[h, 4 * part:4 * part + 4] = total.astype(BF16).reshape(4, 64, 128)
+            for zq in (2 * part, 2 * part + 1):
+                send(gs.at[h, zq * 2 + o], go.at[h, z], s8_s.at[h, zq, 1], s8_r.at[h, z],
+                     place(x, y, c * 4 + zq, o))
+                here = jnp.logical_and(zl == zq, zh == c)
+                src, dst = gs.at[h, zq * 2 + c], go.at[h, z]
+                own = pltpu.make_async_copy(src, dst, s8_r.at[h, z])
+                far = pltpu.make_async_remote_copy(
+                    src_ref=src, dst_ref=dst, send_sem=s8_s.at[h, zq, 0], recv_sem=s8_r.at[h, z],
+                    device_id=place(x, y, c * 4 + zq, c), device_id_type=MESH)
+                pl.when(here)(own.start)
+                pl.when(jnp.logical_not(here))(far.start)
+                far8.append((here, far))
 
     for h in range(2):
         ln = slice(h * 128, (h + 1) * 128)
@@ -445,7 +444,9 @@
     def _():
         for h in range(2):
             far0[h].wait_send()
-            far8[h].wait_send()
+
+    for here, far in far8:
+        pl.when(jnp.logical_not(here))(far.wait_send)
 
 
 def per_device(control, innovation, obs_weight, courant_x, courant_y, filter_x, filter_y):
@@ -485,7 +486,7 @@
         dma(1), dma(1), dma(3), dma(3), dma(4), dma(4),
         dma(2, 8), dma(2, 8), dma(2, 3, 4), dma(2, 3, 4), dma(4, 4, 2), dma(4, 4, 2), dma(8), dma(8),
         dma(8), dma(8), dma(4, 2), dma(4, 2), dma(2), dma(2), dma(7), dma(7), dma(3, 4, 2), dma(3, 4, 2),
-        dma(2, 3), dma(2, 3), dma(2, 4, 2), dma(2, 8),
+        dma(2, 2, 3), dma(2, 2, 3), dma(2, 4, 2), dma(2, 8),
     ]
     out = pltpu.VMEM((64, 8, 256), F32)
     anywhere = pl.BlockSpec(memory_space=pl.ANY)

time: 98.8 us -> 95.3 us (0.965)
  Pallas kernels: 96.5 us -> 92.9 us
    pallas_call x1, Pallas kernels: 96.5 us -> 92.9 us  [per_device(): pl.pallas_call(kernel, out_shape=(out, out), in_specs=[anywhere] * 7, out...]
where the time goes in v6:
time: 95.3 us; the launch traced here: 95.1 us
  Pallas kernels  92.9 us (97%)
  local copies, waits for them, and re-layouts  1.59 us (2%)
    pallas_call x1, Pallas kernels, per_device(): pl.pallas_call(kernel, out_shape=(out, out), in_specs=[anywhere] * 7, out...  92.9 us

profile of v6, /device:TPU:1, one launch (start us, length us, event | category | flops | bytes accessed | tf_op | source)
XLA Modules:
  0.0 95.1 jit_solution(2557073375447897914)
XLA Ops:
  0.6 92.9 %shard_map.86 = (f32[64,8,256]{2,1,0:T(8,128)S(1)}, f32[64,8,256]{2,1,0:T(8,128)S(1)}) custom-call(bf16[64,8,256]{2,1,0:T(8,128)(2,1)} %ctl.1, f32[64,8,256]{2,1,0:T(8,128)} %innov.1, f32[64,8,256]{2,1,0:T(8,128)} %weight.1, f32[64,8,256]{2,1,0:T(8,128)} %cou_x.1, f32[64,8,256]{2,1,0:T(8,128)} %cou_y.1, bf16[4,16,2048]{2,1,0:T(8,128)(2,1)} %bitcast.3, ...), custom_call_target="tpu_custom_call" | custom-call | flops 2150000128 | bytes 5000000 | tf_op jit(solution)/shard_map/pallas_call | solution.py:493
  93.5 0.8 copy.11
  94.3 0.8 copy.12

commit v7 on v6

--- a/solution.py
+++ b/solution.py
@@ -408,6 +408,7 @@
         for part in range(2):
             gown[h, pl.ds(part * 256, 256)] = lines(h, y, part)
 
+    early = len(pending)
     far8 = []
     for h in range(2):
         for part in range(2):
@@ -430,6 +431,14 @@
                 pl.when(jnp.logical_not(here))(far.start)
                 far8.append((here, far))
 
+    for copy in pending[:early]:
+        copy.wait_send()
+
+    @pl.when(zh != c)
+    def _():
+        for h in range(2):
+            far0[h].wait_send()
+
     for h in range(2):
         ln = slice(h * 128, (h + 1) * 128)
         for l in range(8):
@@ -437,13 +446,8 @@
         for l in range(8):
             nat[h, pl.ds(l, 64, stride=8), :] = go[h, l].astype(F32)
         grad_out[:, :, ln] = ctl_v[:, :, ln].astype(F32) + nat[h].reshape(64, 8, 128)
-    for copy in pending:
+    for copy in pending[early:]:
         copy.wait_send()
-
-    @pl.when(zh != c)
-    def _():
-        for h in range(2):
-            far0[h].wait_send()
 
     for here, far in far8:
         pl.when(jnp.logical_not(here))(far.wait_send)

time: 95.3 us -> 95.2 us (level)
  no operation moved by 1% of the time
where the time goes in v7:
time: 95.2 us; the launch traced here: 95 us
  Pallas kernels  92.7 us (97%)
  local copies, waits for them, and re-layouts  1.59 us (2%)
    pallas_call x1, Pallas kernels, per_device(): pl.pallas_call(kernel, out_shape=(out, out), in_specs=[anywhere] * 7, out...  92.7 us

profile of v7, /device:TPU:1, one launch (start us, length us, event | category | flops | bytes accessed | tf_op | source)
XLA Modules:
  0.0 95.0 jit_solution(15048353038227894477)
XLA Ops:
  0.6 92.7 %shard_map.86 = (f32[64,8,256]{2,1,0:T(8,128)S(1)}, f32[64,8,256]{2,1,0:T(8,128)S(1)}) custom-call(bf16[64,8,256]{2,1,0:T(8,128)(2,1)} %ctl.1, f32[64,8,256]{2,1,0:T(8,128)} %innov.1, f32[64,8,256]{2,1,0:T(8,128)} %weight.1, f32[64,8,256]{2,1,0:T(8,128)} %cou_x.1, f32[64,8,256]{2,1,0:T(8,128)} %cou_y.1, bf16[4,16,2048]{2,1,0:T(8,128)(2,1)} %bitcast.3, ...), custom_call_target="tpu_custom_call" | custom-call | flops 2150000128 | bytes 5000000 | tf_op jit(solution)/shard_map/pallas_call | solution.py:497
  93.4 0.8 copy.11
  94.2 0.8 copy.12

commit v8 on v7

--- a/solution.py
+++ b/solution.py
@@ -82,11 +82,13 @@
         pl.semaphore_signal(barrier, inc=1, device_id=dev, device_id_type=MESH)
 
     load_ctl.wait()
-    for h in range(2):
+
+    def by_level(h):
         nat[h] = ctl_v[:, :, h * 128:(h + 1) * 128].astype(F32).reshape(512, 128)
-    for l in range(8):
-        for h in range(2):
+        for l in range(8):
             snd0[h, l] = nat[h, pl.ds(l, 64, stride=8), :].astype(BF16)
+
+    by_level(0)
 
     pl.semaphore_wait(barrier, len(partners))
 
@@ -94,6 +96,8 @@
     x2 = xs[2]
     own0, far0 = [], []
     for h in range(2):
+        if h:
+            by_level(1)
         for t in (4, 3, 5, 2, 6, 1, 7):
             send(snd0.at[h, zs[t]], cg.at[h, gx], s0_s.at[h, t], s0_r.at[h, slot0], place(x, y, zs[t], zh))
         src, dst = snd0.at[h, z], cg.at[h, gx]

time: 95.2 us -> 95.2 us (level)
  no operation moved by 1% of the time
where the time goes in v8:
time: 95.2 us; the launch traced here: 95 us
  Pallas kernels  92.7 us (97%)
  local copies, waits for them, and re-layouts  1.59 us (2%)
    pallas_call x1, Pallas kernels, per_device(): pl.pallas_call(kernel, out_shape=(out, out), in_specs=[anywhere] * 7, out...  92.7 us

profile of v8, /device:TPU:1, one launch (start us, length us, event | category | flops | bytes accessed | tf_op | source)
XLA Modules:
  0.0 95.0 jit_solution(11402013059481589769)
XLA Ops:
  0.6 92.7 %shard_map.86 = (f32[64,8,256]{2,1,0:T(8,128)S(1)}, f32[64,8,256]{2,1,0:T(8,128)S(1)}) custom-call(bf16[64,8,256]{2,1,0:T(8,128)(2,1)} %ctl.1, f32[64,8,256]{2,1,0:T(8,128)} %innov.1, f32[64,8,256]{2,1,0:T(8,128)} %weight.1, f32[64,8,256]{2,1,0:T(8,128)} %cou_x.1, f32[64,8,256]{2,1,0:T(8,128)} %cou_y.1, bf16[4,16,2048]{2,1,0:T(8,128)(2,1)} %bitcast.3, ...), custom_call_target="tpu_custom_call" | custom-call | flops 2150000128 | bytes 5000000 | tf_op jit(solution)/shard_map/pallas_call | solution.py:501
  93.4 0.8 copy.11
  94.2 0.8 copy.12
